TPU v7x, 512 devices: a whole 4x8x8 slice. The times are simulated.
512 devices in a mesh: row: 64 (over z_lo, x, y), col: 8 (over z_hi, core).
Axes of the slice: x: 4, y: 8, z: 8 (z_hi: 4, z_lo: 2; z = z_hi * 2 + z_lo), core: 2. Of those that a mesh axis runs over, the one named last changes fastest.
Arguments:
- slab: float32 [4096, 8192], P('row', 'col')
- pairing: int32 [2, 8], replicated, may hold values from 0 to 2, as said below
Outputs:
- rotated: float32 [4096, 8192], P('row', 'col')
Inputs may be any that keep to these rules, and one draw needn't show every extreme that they name: `pairing`: each entry names one of the three pairings of a group's slots.
All inputs are finite; a program needn't handle non-finite values.
Results may differ from a plain program's by a relative error of at most 0.00045.
Values sent between devices are 32-bit elements; how exact they have to be, the bound alone decides.
No kernel may reach another device: no remote copies, remote signals or barrier semaphores. Data moves between devices by JAX's collectives and lax.ppermute only.
A program may use at most 64 MiB of HBM per device.

v0:
```python
import jax
import jax.numpy as jnp
from jax import lax
from jax.sharding import PartitionSpec as P

ROUNDS = 2


EPS = 1e-06
ORDERS = ((0, 1, 2, 3), (0, 2, 1, 3), (0, 3, 1, 2))
RESTORE = ((0, 1, 2, 3), (0, 2, 1, 3), (0, 2, 3, 1))


def from_behind(value, axis, by):
    count = lax.axis_size(axis)
    return lax.ppermute(value, axis, [(i, (i + by) % count) for i in range(count)])


def arrange(blocks, which, tables):
    branches = [
        lambda b, order=order: jnp.stack([b[:, i] for i in order], axis=1) for order in tables
    ]
    return lax.switch(which, branches, blocks)


def inverse_of(matrix, eye):
    factor = jnp.linalg.cholesky(matrix)
    lower_inv = lax.linalg.triangular_solve(factor, eye, left_side=True, lower=True)
    return jnp.dot(lower_inv.T, lower_inv, precision=lax.Precision.HIGHEST)


def rotate(first, second, cross, norm_first, norm_second, eye):
    high = lax.Precision.HIGHEST
    coupling = cross * lax.rsqrt(norm_first + EPS)[:, None] * lax.rsqrt(norm_second + EPS)[None, :]
    p_inv = inverse_of(eye + jnp.dot(coupling, coupling.T, precision=high), eye)
    q_inv = inverse_of(eye + jnp.dot(coupling.T, coupling, precision=high), eye)
    top = jnp.concatenate(
        [2.0 * p_inv - eye, 2.0 * jnp.dot(p_inv, coupling, precision=high)], axis=1
    )
    bottom = jnp.concatenate(
        [-2.0 * jnp.dot(q_inv, coupling.T, precision=high), 2.0 * q_inv - eye], axis=1
    )
    rotation = jnp.concatenate([top, bottom], axis=0)
    joined = jnp.concatenate([first, second], axis=1)
    result = jnp.dot(joined, rotation, precision=high)
    width = first.shape[1]
    return (result[:, :width], result[:, width:])


def whole_gram(first, second):
    joined = jnp.concatenate([first, second], axis=1)
    return jnp.dot(joined.T, joined, precision=lax.Precision.HIGHEST)


def split_gram(gram, width):
    diagonal = jnp.diagonal(gram)
    return (gram[:width, width:], diagonal[:width], diagonal[width:])


def local(slab, pairing):
    rows = slab.shape[0]
    width = slab.shape[1] // 4
    blocks = slab.reshape(rows, 4, width)
    group = lax.axis_index("col")
    eye = jnp.eye(width, dtype=jnp.float32)
    for step in range(ROUNDS):
        which = pairing[step, group]
        ordered = arrange(blocks, which, ORDERS)
        first_a = ordered[:, 0]
        second_a = ordered[:, 1]
        first_b = ordered[:, 2]
        second_b = ordered[:, 3]
        gram_a, gram_b = lax.psum(
            (whole_gram(first_a, second_a), whole_gram(first_b, second_b)), "row"
        )
        stats_a = split_gram(gram_a, width)
        stats_b = split_gram(gram_b, width)
        new_fa, new_sa = rotate(first_a, second_a, *stats_a, eye)
        new_fb, new_sb = rotate(first_b, second_b, *stats_b, eye)
        stacked = jnp.stack([new_fa, new_sa, new_fb, new_sb], axis=1)
        blocks = arrange(stacked, which, RESTORE)
        if step + 1 < ROUNDS:
            ahead = from_behind(blocks[:, 1], "col", 1)
            behind = from_behind(blocks[:, 3], "col", -1)
            blocks = jnp.stack([blocks[:, 0], ahead, blocks[:, 2], behind], axis=1)
    return blocks.reshape(rows, 4 * width)


def solution(mesh):
    in_specs = (P("row", "col"), P())
    out_specs = P("row", "col")
    return jax.shard_map(local, mesh=mesh, in_specs=in_specs, out_specs=out_specs, check_vma=False)
```

profile of v0, /device:TPU:136, one launch (start us, length us, event | category | flops | bytes accessed | tf_op | source)
XLA Modules:
  0.0 1863.9 jit_solution(13789940266584935294)
XLA Ops:
  15.1 618.1 %all-reduce.8.cloned.1.call-done = (f32[512,512]{1,0:T(8,128)}, f32[512,512]{1,0:T(8,128)}) async-done(((f32[512,512]{1,0:T(8,128)}, f32[512,512]{1,0:T(8,128)}), (f32[512,512]{1,0:T(8,128)}, f32[512,512]{1,0:T(8,128)})) %all-reduce.8.cloned.1.call-update) | async-done | bytes 2097168 | tf_op jit(solution)/shard_map/psum | solution.py:73
  633.2 8.7 gather_fusion.1
  643.2 4.7 gather_fusion
  651.7 11.7 cholesky.450
  664.6 10.6 custom-call.37
  678.1 12.5 cholesky.467
  695.7 5.5 while.18
  696.4 2.1 bitcast_dynamic-update-slice_fusion.18
  701.2 21.5 %custom-call.38 = f32[2,128,128]{1,2,0:T(8,128)} custom-call(f32[2,128,128]{2,1,0:T(8,128)} %get-tuple-element.188), custom_call_target="InvertDiagBlocksLowerTriangular" | custom-call | tf_op jit(solution)/shard_map/triangular_solve/custom-call.0 | solution.py:28
  729.3 11.7 cholesky.484
  742.2 10.6 custom-call.39
  754.0 12.7 cholesky.501
  770.6 4.0 while.19
  774.6 19.7 %custom-call.40 = f32[2,128,128]{1,2,0:T(8,128)S(1)} custom-call(f32[2,128,128]{2,1,0:T(8,128)S(1)} %get-tuple-element.189), custom_call_target="InvertDiagBlocksLowerTriangular" | custom-call | tf_op jit(solution)/shard_map/triangular_solve/custom-call.0 | solution.py:28
  798.9 11.7 cholesky.382
  810.7 9.8 custom-call.33
  821.0 12.1 cholesky.399
  835.8 4.0 while.16
  839.8 19.7 %custom-call.34 = f32[2,128,128]{1,2,0:T(8,128)S(1)} custom-call(f32[2,128,128]{2,1,0:T(8,128)S(1)} %get-tuple-element.186), custom_call_target="InvertDiagBlocksLowerTriangular" | custom-call | tf_op jit(solution)/shard_map/triangular_solve/custom-call.0 | solution.py:28
  862.0 11.7 cholesky.416
  873.7 9.8 custom-call.35
  884.0 11.7 cholesky.433
  898.6 4.0 while.17
  902.6 19.7 %custom-call.36 = f32[2,128,128]{1,2,0:T(8,128)S(1)} custom-call(f32[2,128,128]{2,1,0:T(8,128)S(1)} %get-tuple-element.187), custom_call_target="InvertDiagBlocksLowerTriangular" | custom-call | tf_op jit(solution)/shard_map/triangular_solve/custom-call.0 | solution.py:28
  928.6 4.5 collective-permute-start.1
  940.7 615.9 %all-reduce.6.cloned.1.call-done = (f32[512,512]{1,0:T(8,128)}, f32[512,512]{1,0:T(8,128)}) async-done(((f32[512,512]{1,0:T(8,128)}, f32[512,512]{1,0:T(8,128)}), (f32[512,512]{1,0:T(8,128)}, f32[512,512]{1,0:T(8,128)})) %all-reduce.6.cloned.1.call-update) | async-done | bytes 2097168 | tf_op jit(solution)/shard_map/psum | solution.py:73
  1556.6 8.7 gather_fusion.3
  1566.6 4.9 gather_fusion.2
  1575.3 11.7 cholesky.586
  1589.6 11.3 custom-call.45
  1603.7 13.2 cholesky.603
  1622.7 6.6 while.22
  1629.3 21.2 %custom-call.46 = f32[2,128,128]{1,2,0:T(8,128)} custom-call(f32[2,128,128]{2,1,0:T(8,128)} %get-tuple-element.192), custom_call_target="InvertDiagBlocksLowerTriangular" | custom-call | tf_op jit(solution)/shard_map/triangular_solve/custom-call.0 | solution.py:28
  1656.4 11.7 cholesky.620
  1670.8 11.3 custom-call.47
  1684.0 12.9 cholesky.637
  1700.9 4.0 while.23
  1704.9 19.7 %custom-call.48 = f32[2,128,128]{1,2,0:T(8,128)S(1)} custom-call(f32[2,128,128]{2,1,0:T(8,128)S(1)} %get-tuple-element.193), custom_call_target="InvertDiagBlocksLowerTriangular" | custom-call | tf_op jit(solution)/shard_map/triangular_solve/custom-call.0 | solution.py:28
  1728.6 11.7 cholesky.518
  1740.4 9.8 custom-call.41
  1750.7 11.9 cholesky.535
  1766.0 4.1 while.20
  1770.1 19.7 %custom-call.42 = f32[2,128,128]{1,2,0:T(8,128)S(1)} custom-call(f32[2,128,128]{2,1,0:T(8,128)S(1)} %get-tuple-element.190), custom_call_target="InvertDiagBlocksLowerTriangular" | custom-call | tf_op jit(solution)/shard_map/triangular_solve/custom-call.0 | solution.py:28
  1792.3 11.7 cholesky.552
  1804.0 9.8 custom-call.43
  1814.3 11.7 cholesky.569
  1828.8 3.8 while.21
  1832.6 19.7 %custom-call.44 = f32[2,128,128]{1,2,0:T(8,128)S(1)} custom-call(f32[2,128,128]{2,1,0:T(8,128)S(1)} %get-tuple-element.191), custom_call_target="InvertDiagBlocksLowerTriangular" | custom-call | tf_op jit(solution)/shard_map/triangular_solve/custom-call.0 | solution.py:28
  (343 shorter events, 134.4 us)
Async XLA Ops:
  6.5 626.6 %all-reduce.8.cloned.1.call-start = ((), (), s32[]{:S(2)}) async-start(), calls=%async_computation.1 | async-start | bytes 4194304 | tf_op jit(solution)/shard_map/psum | solution.py:73
  7.6 0.7 copy-start.34
  9.9 2.6 copy-start.27
  9.9 2.6 copy-start.23
  14.5 1542.1 %all-reduce.6.cloned.1.call-start = ((), (), s32[]{:S(2)}) async-start(), calls=%async_computation | async-start | bytes 4194304 | tf_op jit(solution)/shard_map/psum | solution.py:73
  633.2 8.8 copy-start.2
  641.9 1.3 copy-start
  651.0 0.7 copy-start.6
  690.7 3.3 copy-start.4
  691.4 0.7 copy-start.35
  694.0 1.0 copy-start.45
  701.2 21.5 %copy-start.39 = (s32[2,2]{1,0:T(2,128)}, s32[2,2]{1,0:T(2,128)S(1)}, u32[]{:S(2)}) copy-start(s32[2,2]{1,0:T(2,128)S(1)} %get-tuple-element.821) | copy-start | bytes 52
  723.8 0.9 copy-start.29
  726.3 0.7 copy-start.32
  728.6 0.7 copy-start.7
  729.3 23.6 %copy-start.8 = (f32[256,256]{1,0:T(8,128)S(1)}, f32[256,256]{1,0:T(8,128)}, u32[]{:S(2)}) copy-start(f32[256,256]{1,0:T(8,128)} %copy-done.7) | copy-start | bytes 786436
  767.4 0.6 copy-start.36
  769.9 0.7 copy-start.40
  795.9 0.7 copy-start.33
  796.6 0.9 copy-start.12
  796.6 1.0 copy-start.14
  796.6 1.0 copy-start.26
  796.6 1.0 copy-start.28
  902.6 19.7 %copy-start.41 = (s32[2,2]{1,0:T(2,128)}, s32[2,2]{1,0:T(2,128)S(1)}, u32[]{:S(2)}) copy-start(s32[2,2]{1,0:T(2,128)S(1)} %get-tuple-element.824) | copy-start | bytes 52
  923.9 0.8 copy-start.24
  926.7 7.1 collective-permute-start
  928.6 6.8 collective-permute-start.1
  936.0 0.6 copy-start.18
  1556.6 8.8 copy-start.3
  1565.3 1.2 copy-start.1
  1574.5 0.7 copy-start.9
  1587.0 0.6 copy-start.20
  1617.8 3.2 copy-start.5
  1618.5 0.6 copy-start.37
  1622.7 0.7 copy-start.42
  1626.0 0.7 copy-start.42
  1651.7 0.9 copy-start.30
  1655.7 0.7 copy-start.10
  1656.4 25.7 %copy-start.11 = (f32[256,256]{1,0:T(8,128)S(1)}, f32[256,256]{1,0:T(8,128)}, u32[]{:S(2)}) copy-start(f32[256,256]{1,0:T(8,128)} %copy-done.10) | copy-start | bytes 786436
  1668.2 0.6 copy-start.21
  1697.7 0.6 copy-start.38
  1700.3 0.7 copy-start.43
  1726.2 1.0 copy-start.13
  1726.2 1.0 copy-start.15
  1726.2 1.0 copy-start.17
  1726.3 1.0 copy-start.19
  1765.3 0.7 copy-start.44
  1856.1 0.7 copy-start.22
  (3 other events, 1.8 us)
Sparse Core Ops, SparseCore 0:
  14.6 618.5 all-reduce.7
  940.8 615.7 all-reduce.5
where the time goes:
time: 1870 us; the launch traced here: 1860 us
  waiting for transfers between devices  1240 us (66%)
  other arithmetic  459 us (25%)
  local copies, waits for them, and re-layouts  86.6 us (5%)
  matrix products  49.4 us (3%)
  between operations  26.6 us (1%)
    psum x2, waiting for transfers between devices, local(): lax.psum((whole_gram(first_a, second_a), whole_gram(first_b, second_b)),...  1230 us
    another operation x56, other arithmetic, inverse_of(): factor = jnp.linalg.cholesky(matrix)  292 us
    another operation x17, other arithmetic, inverse_of(): lax.linalg.triangular_solve(factor, eye, left_side=True, lower=True)  163 us
  transfers between devices with their start and end apart: 4, of which 3 were waited for; matrix products, arithmetic and copies ran while one was open for 0% of the time, Pallas kernels for 0%

commit v1 on v0

v1 whole, which is shorter than its diff:
```python
import functools
import math

import jax
import jax.numpy as jnp
from jax import lax
from jax.experimental import pallas as pl
from jax.experimental.pallas import tpu as pltpu
from jax.sharding import Mesh, PartitionSpec as P

EPS = 1e-06
WIDTH = 256
HALF = 128
ROWS = 64
CHUNKS = 16
PART = WIDTH // CHUNKS
NORMS = 4 * PART
OUTER = ("z_lo", "x", "y_lo")
RING = ("y_hi",)
COL = ("z_hi", "core")

NT = (((1,), (1,)), ((), ()))
NN = (((1,), (0,)), ((), ()))
TN = (((0,), (0,)), ((), ()))


TOLERANCE = 2e-6


def step_table():
    table = []
    steps = 32
    while not table or table[-1][1] < 70000.0:
        low, high = 0.0, 1e6
        for _ in range(80):
            b = 0.5 * (low + high)
            root = 2.0 * math.sqrt(1.0 + b) / (2.0 + b)
            rho = b / (2.0 + b) / (1.0 + root)
            error = rho ** (steps + 1) * (1.0 + (steps + 1) * root)
            low, high = (b, high) if error < TOLERANCE else (low, b)
        table.append((steps, low))
        steps = (steps * 5) // 4
    return fourth(table)


def squaring_table():
    table = []
    for count in range(1, 7):
        mu = TOLERANCE ** (0.5 ** (count + 2))
        table.append((count, 2.0 * mu / (1.0 - mu)))
    return fourth(table)


def fourth(table):
    return [(count, (limit / 1.001) ** 4) for count, limit in table]


def count_of(bound, table):
    count = table[0][0]
    for (_, limit), (more, _) in zip(table[:-1], table[1:]):
        count = jnp.where(bound > limit, more, count)
    return count


STEPS = step_table()
SQUARINGS = squaring_table()


def halves(a):
    high = a.astype(jnp.bfloat16)
    return high, (a - high.astype(jnp.float32)).astype(jnp.bfloat16)


def stack(a, b):
    return tuple(jnp.concatenate(p, axis=0) for p in zip(a, b))


def dot3(a, b, dims):
    ah, al = a
    bh, bl = b
    dot = lambda u, v: lax.dot_general(u, v, dims, preferred_element_type=jnp.float32)
    return dot(ah, bh) + (dot(ah, bl) + dot(al, bh))


def slots_of(which):
    first_b = jnp.where(which == 0, 2, 1)
    second_b = jnp.where(which == 2, 2, 3)
    return ((0, which + 1), (first_b, second_b))


def pick(pairing_ref, step):
    return pairing_ref[step, lax.axis_index(COL)]


def load_blocks(refs, blocks):
    for s in range(4):
        blocks[s] = refs[0][:, s * WIDTH : (s + 1) * WIDTH] if len(refs) == 1 else refs[s][...]


def gram_kernel(step, pairing_ref, *refs):
    *ins, out, blocks = refs
    load_blocks(ins, blocks)
    for c in range(1, CHUNKS):
        out[c, NORMS:] = jnp.zeros((8, HALF), jnp.float32)
    for pair, (f, s) in enumerate(slots_of(pick(pairing_ref, step))):
        x = blocks[f]
        y = blocks[s]
        cross = dot3(halves(x), halves(y), TN)
        for side, block in enumerate((x, y)):
            norm = jnp.sum(block * block, axis=0, keepdims=True)
            for h in range(2):
                row = NORMS + 4 * pair + 2 * side + h
                out[0, row : row + 1] = norm[:, h * HALF : (h + 1) * HALF]
        for h in range(2):
            start = (2 * pair + h) * PART
            half = cross[:, h * HALF : (h + 1) * HALF]
            out[:, start : start + PART, :] = half.reshape(CHUNKS, PART, HALF)


def sum_kernel(parts, out):
    total = parts[0]
    for c in range(1, parts.shape[0]):
        total = total + parts[c]
    for c in range(out.shape[0]):
        out[c] = total


def turn_kernel(step, pairing_ref, gram, *refs):
    count = 1 if step == 0 else 4
    ins, outs, (blocks, coupling, powers, solved) = refs[:count], refs[count:-4], refs[-4:]
    load_blocks(ins, blocks)
    pairs = slots_of(pick(pairing_ref, step))
    scale = lax.rsqrt(gram[0, NORMS:] + EPS)
    scale_t = scale.T
    xs, ys, cs, ms, ts, starts, squares = [], [], [], [], [], [], []
    bound = None
    for pair, (f, s) in enumerate(pairs):
        x = blocks[f]
        y = blocks[s]
        row = 4 * pair
        down = jnp.concatenate([scale_t[:, row : row + 1], scale_t[:, row + 1 : row + 2]], axis=0)
        sides = []
        for h in range(2):
            start = (2 * pair + h) * PART
            half = gram[:, start : start + PART, :].reshape(WIDTH, HALF)
            sides.append(half * down * scale[row + 2 + h : row + 3 + h])
        coupling[pair] = jnp.concatenate(sides, axis=1)
        c = halves(coupling[pair])
        both = dot3(stack(halves(y), c), c, NT)
        t = x - both[:ROWS]
        m = both[ROWS:]
        mh = halves(m)
        both = dot3(stack(halves(t), mh), mh, NN)
        square = both[ROWS:]
        most = jnp.sum(square * square)
        bound = most if bound is None else jnp.maximum(bound, most)
        xs.append(x)
        ys.append(y)
        cs.append(c)
        ms.append(m)
        ts.append(t)
        starts.append(both[:ROWS])
        squares.append(square)
    b = jnp.sqrt(jnp.sqrt(jnp.full((8, 128), bound, jnp.float32)))[:1, :1] * 1.001

    @pl.when(bound <= SQUARINGS[-1][1])
    def _():
        relax = 2.0 / (2.0 + b)
        keep = 0.5 * b * relax
        diagonal = lax.broadcasted_iota(jnp.int32, (WIDTH, WIDTH), 0) == lax.broadcasted_iota(
            jnp.int32, (WIDTH, WIDTH), 1
        )
        for pair in range(2):
            off = (relax * relax) * squares[pair] - (2.0 * keep * relax) * ms[pair]
            powers[pair] = jnp.where(diagonal, off + keep * keep, off)
            solved[pair] = relax * ((1.0 + keep) * ts[pair] - relax * starts[pair])

        def body(_, carry):
            for pair in range(2):
                z = solved[pair]
                r = halves(powers[pair])
                both = dot3(stack(halves(z), r), r, NN)
                solved[pair] = z + both[:ROWS]
                powers[pair] = both[ROWS:]
            return carry

        lax.fori_loop(0, count_of(bound, SQUARINGS), body, 0)
        for pair, ((f, s), x, y, c) in enumerate(zip(pairs, xs, ys, cs)):
            z = solved[pair]
            z = z + dot3(halves(z), halves(powers[pair]), NN)
            blocks[f] = 2.0 * z - x
            blocks[s] = y + 2.0 * dot3(halves(z), c, NN)

    @pl.when(bound > SQUARINGS[-1][1])
    def _():
        dot = functools.partial(
            lax.dot_general, precision=lax.Precision.HIGHEST, preferred_element_type=jnp.float32
        )
        relax = 2.0 / (2.0 + b)
        omega = 2.0 / (1.0 + relax * jnp.sqrt(1.0 + b))
        gain = omega * relax
        for pair, (f, s) in enumerate(pairs):
            x = blocks[f]
            y = blocks[s]
            c = coupling[pair]
            t = x - dot(y, c, NT)
            powers[pair] = dot(c, c, NT)

            def body(_, carry):
                z, before = carry
                residual = t - z - dot(z, powers[pair], NN)
                return before + omega * (z - before) + gain * residual, z

            z, _ = lax.fori_loop(0, count_of(bound, STEPS), body, (relax * t, jnp.zeros_like(t)))
            blocks[f] = 2.0 * z - x
            blocks[s] = y + 2.0 * dot(z, c, NN)

    for s in range(4):
        if len(outs) == 1:
            outs[0][:, s * WIDTH : (s + 1) * WIDTH] = blocks[s]
        else:
            outs[s][...] = blocks[s]


SMEM = pl.BlockSpec(memory_space=pltpu.SMEM)
VMEM = pl.BlockSpec(memory_space=pltpu.VMEM)
BLOCKS = pltpu.VMEM((4, ROWS, WIDTH), jnp.float32)
PARAMS = pltpu.CompilerParams(vmem_limit_bytes=8 * 2**20)


def shape(*sizes):
    return jax.ShapeDtypeStruct(sizes, jnp.float32)


def gram_of(step, pairing, ins):
    return pl.pallas_call(
        lambda *refs: gram_kernel(step, *refs),
        out_shape=shape(CHUNKS, NORMS + 8, HALF),
        in_specs=[SMEM] + [VMEM] * len(ins),
        out_specs=VMEM,
        scratch_shapes=[BLOCKS],
        compiler_params=PARAMS,
        name="gram",
    )(pairing, *ins)


def add_up(parts, copies):
    return pl.pallas_call(
        sum_kernel,
        out_shape=shape(copies, *parts.shape[1:]),
        in_specs=[VMEM],
        out_specs=VMEM,
        compiler_params=PARAMS,
        name="add_up",
    )(parts)


def turn(step, pairing, gram, ins):
    outs = [shape(ROWS, WIDTH)] * 4 if step == 0 else shape(ROWS, 4 * WIDTH)
    return pl.pallas_call(
        lambda *refs: turn_kernel(step, *refs),
        out_shape=outs,
        in_specs=[SMEM] + [VMEM] * (1 + len(ins)),
        out_specs=[VMEM] * 4 if step == 0 else VMEM,
        scratch_shapes=[
            BLOCKS,
            pltpu.VMEM((2, WIDTH, WIDTH), jnp.float32),
            pltpu.VMEM((2, WIDTH, WIDTH), jnp.float32),
            pltpu.VMEM((2, ROWS, WIDTH), jnp.float32),
        ],
        compiler_params=PARAMS,
        name="turn",
    )(pairing, gram, *ins)


def whole(parts):
    parts = add_up(lax.all_to_all(parts, OUTER, 0, 0), lax.axis_size(RING))
    parts = add_up(lax.all_to_all(parts, RING, 0, 0), CHUNKS)
    return lax.all_to_all(parts, OUTER, 0, 0)


def local(slab, pairing):
    ins = (slab,)
    gram = whole(gram_of(0, pairing, ins))
    stay, ahead, wait, behind = turn(0, pairing, gram, ins)
    ahead = lax.ppermute(ahead, COL, [(i, (i + 1) % 8) for i in range(8)])
    behind = lax.ppermute(behind, COL, [(i, (i - 1) % 8) for i in range(8)])
    ins = (stay, ahead, wait, behind)
    gram = whole(gram_of(1, pairing, ins))
    return turn(1, pairing, gram, ins)


def solution(mesh):
    names = ("z_lo", "x", "y_hi", "y_lo", "z_hi", "core")
    fine = Mesh(mesh.devices.reshape(2, 4, 4, 2, 4, 2), names)
    spec = P(names[:4], COL)
    return jax.shard_map(local, mesh=fine, in_specs=(spec, P()), out_specs=spec, check_vma=False)
```

time: 1870 us -> 609 us (0.33)
  the two profiles are of different devices: /device:TPU:136 before, /device:TPU:129 now
where the time goes in v1:
time: 609 us
  Pallas kernels  518 us (85%)
  blocking collectives  79 us (13%)
    pallas_call x2, Pallas kernels, turn(): pl.pallas_call(lambda *refs: turn_kernel(step, *refs), out_shape=outs, in...  516 us
    all_to_all x2, blocking collectives, whole(): parts = add_up(lax.all_to_all(parts, OUTER, 0, 0), lax.axis_size(RING))  28.9 us
    all_to_all x2, blocking collectives, whole(): return lax.all_to_all(parts, OUTER, 0, 0)  26.7 us
    all_to_all x2, blocking collectives, whole(): parts = add_up(lax.all_to_all(parts, RING, 0, 0), CHUNKS)  23.4 us
  transfers between devices with their start and end apart: 2, of which 1 were waited for; matrix products, arithmetic and copies ran while one was open for 0% of the time, Pallas kernels for 0%

profile of v1, /device:TPU:129, one launch (start us, length us, event | category | flops | bytes accessed | tf_op | source)
XLA Modules:
  0.0 609.0 jit_solution(779709346669071130)
XLA Ops:
  0.0 0.0 copy-start
  0.0 0.9 copy-done
  1.0 0.0 copy-start.2
  1.0 0.7 copy-done.2
  1.6 1.0 gram.2
  2.6 17.2 %all_to_all.30.parts = f32[16,72,128]{2,1,0:T(8,128)S(1)} all-to-all(f32[16,72,128]{2,1,0:T(8,128)S(1)} %gram.2), channel_id=1, replica_groups=mesh['z_lo'=2,'x'=4,'y_hi'=4,'y_lo'=2,'z_hi'=4,'core'=2] {'z_lo','x','y_..., dimensions={0} | all-to-all | bytes 1179648 | tf_op jit(solution)/shard_map/all_to_all | solution.py:277
  19.9 13.8 %all_to_all.31.parts = f32[4,72,128]{2,1,0:T(8,128)S(1)} all-to-all(f32[4,72,128]{2,1,0:T(8,128)S(1)} %add_up.4), channel_id=1, replica_groups=mesh['z_lo'=2,'x'=4,'y_hi'=4,'y_lo'=2,'z_hi'=4,'core'=2] {'y_hi'}, dimensions={0} | all-to-all | bytes 294912 | tf_op jit(solution)/shard_map/all_to_all | solution.py:278
  33.7 0.0 copy-start.1
  33.7 0.0 copy-start.3
  33.7 11.5 %all_to_all.32.refs_1_ = f32[16,72,128]{2,1,0:T(8,128)S(1)} all-to-all(f32[16,72,128]{2,1,0:T(8,128)S(1)} %add_up.5), channel_id=1, replica_groups=mesh['z_lo'=2,'x'=4,'y_hi'=4,'y_lo'=2,'z_hi'=4,'core'=2] {'z_lo','x','y_..., dimensions={0} | all-to-all | bytes 1179648 | tf_op jit(solution)/shard_map/all_to_all | solution.py:279
  45.2 0.0 copy-done.1
  45.2 0.0 copy-done.3
  45.2 229.5 %turn.2 = (f32[64,256]{1,0:T(8,128)S(1)}, f32[64,256]{1,0:T(8,128)S(1)}, f32[64,256]{1,0:T(8,128)S(1)}, f32[64,256]{1,0:T(8,128)S(1)}) custom-call(s32[2,8]{1,0:T(2,128)S(1)} %copy-done.3, f32[16,72,128]{2,1,0:T(8,128)S(1)} %all_to_all.32.refs_1_, f32[64,1024]{1,0:T(8,128)S(1)} %copy-done.1), custom_call_target="tpu_custom_call" | custom-call | tf_op jit(solution)/shard_map/turn/pallas_call | solution.py:260
  274.7 1.9 collective-permute-start
  276.6 2.4 collective-permute-start.1
  279.0 0.0 collective-permute-done.refs_2_.refs_3_
  279.0 6.0 collective-permute-done.1.refs_4_.refs_5_
  285.0 1.0 gram.3
  286.0 11.6 %all_to_all.33.parts = f32[16,72,128]{2,1,0:T(8,128)S(1)} all-to-all(f32[16,72,128]{2,1,0:T(8,128)S(1)} %gram.3), channel_id=1, replica_groups=mesh['z_lo'=2,'x'=4,'y_hi'=4,'y_lo'=2,'z_hi'=4,'core'=2] {'z_lo','x','y_..., dimensions={0} | all-to-all | bytes 1179648 | tf_op jit(solution)/shard_map/all_to_all | solution.py:277
  297.7 9.7 %all_to_all.34.parts = f32[4,72,128]{2,1,0:T(8,128)S(1)} all-to-all(f32[4,72,128]{2,1,0:T(8,128)S(1)} %add_up.6), channel_id=1, replica_groups=mesh['z_lo'=2,'x'=4,'y_hi'=4,'y_lo'=2,'z_hi'=4,'core'=2] {'y_hi'}, dimensions={0} | all-to-all | bytes 294912 | tf_op jit(solution)/shard_map/all_to_all | solution.py:278
  307.4 15.2 %all_to_all.35.refs_1_ = f32[16,72,128]{2,1,0:T(8,128)S(1)} all-to-all(f32[16,72,128]{2,1,0:T(8,128)S(1)} %add_up.7), channel_id=1, replica_groups=mesh['z_lo'=2,'x'=4,'y_hi'=4,'y_lo'=2,'z_hi'=4,'core'=2] {'z_lo','x','y_..., dimensions={0} | all-to-all | bytes 1179648 | tf_op jit(solution)/shard_map/all_to_all | solution.py:279
  322.6 286.4 %turn.3 = f32[64,1024]{1,0:T(8,128)} custom-call(s32[2,8]{1,0:T(2,128)S(1)} %copy-done.3, f32[16,72,128]{2,1,0:T(8,128)S(1)} %all_to_all.35.refs_1_, f32[64,256]{1,0:T(8,128)S(1)} %get-tuple-element.9.refs_1_.refs_2_, f32[64,256]{1,0:T(8,128)S(1)} %collective-permute-done.refs_2_.refs_3_, f32[64,256]{1,0:T(8,128)S(1)} %get-tuple-element.11.refs_3_.refs_4_, ...), custom_call_target="tpu_custom_call" | custom-call | tf_op jit(solution)/shard_map/turn/pallas_call | solution.py:260
  (4 shorter events, 0.2 us)
Async XLA Ops:
  0.0 0.9 copy-start
  1.0 0.7 copy-start.2
  33.7 11.5 %copy-start.1 = (f32[64,1024]{1,0:T(8,128)S(1)}, f32[64,1024]{1,0:T(8,128)}, u32[]{:S(2)}) copy-start(f32[64,1024]{1,0:T(8,128)} %refs_2_.1) | copy-start | bytes 786436
  33.7 11.5 %copy-start.3 = (s32[2,8]{1,0:T(2,128)S(1)}, s32[2,8]{1,0:T(2,128)}, u32[]{:S(2)}) copy-start(s32[2,8]{1,0:T(2,128)} %refs_0_.7) | copy-start | bytes 196
  274.7 4.3 collective-permute-start
  276.6 8.4 %collective-permute-start.1 = (f32[64,256]{1,0:T(8,128)S(1)}, f32[64,256]{1,0:T(8,128)S(1)}, u32[]{:S(2)}, u32[]{:S(2)}) collective-permute-start(f32[64,256]{1,0:T(8,128)S(1)} %get-tuple-element.12), channel_id=1, source_target_pairs={{0,7},{1,0},{2,1},{3,2},{4,3},{5,4},{6,5},{7,6},{8,15},{9,8},{10,9... | collective-permute-start | bytes 196616 | tf_op jit(solution)/shard_map/ppermute | solution.py:287

commit v2 on v1

--- a/solution.py
+++ b/solution.py
@@ -18,6 +18,7 @@
 OUTER = ("z_lo", "x", "y_lo")
 RING = ("y_hi",)
 COL = ("z_hi", "core")
+CORE = "core"
 
 NT = (((1,), (1,)), ((), ()))
 NN = (((1,), (0,)), ((), ()))
@@ -25,6 +26,7 @@
 
 
 TOLERANCE = 2e-6
+CUBIC_TOLERANCE = 1e-5
 
 
 def step_table():
@@ -44,9 +46,11 @@
 
 
 def squaring_table():
+    rho = (0.5 * CUBIC_TOLERANCE) ** 0.25
+    top = 4.0 * rho / (1.0 + rho) ** 2
     table = []
     for count in range(1, 7):
-        mu = TOLERANCE ** (0.5 ** (count + 2))
+        mu = top ** (0.5**count)
         table.append((count, 2.0 * mu / (1.0 - mu)))
     return fourth(table)
 
@@ -71,15 +75,12 @@
     return high, (a - high.astype(jnp.float32)).astype(jnp.bfloat16)
 
 
-def stack(a, b):
-    return tuple(jnp.concatenate(p, axis=0) for p in zip(a, b))
-
-
-def dot3(a, b, dims):
-    ah, al = a
-    bh, bl = b
+def dots3(operands, dims):
     dot = lambda u, v: lax.dot_general(u, v, dims, preferred_element_type=jnp.float32)
-    return dot(ah, bh) + (dot(ah, bl) + dot(al, bh))
+    tops = [dot(a[0], b[0]) for a, b in operands]
+    lows = [dot(a[0], b[1]) for a, b in operands]
+    highs = [dot(a[1], b[0]) for a, b in operands]
+    return [t + (l + h) for t, l, h in zip(tops, lows, highs)]
 
 
 def slots_of(which):
@@ -89,12 +90,34 @@
 
 
 def pick(pairing_ref, step):
-    return pairing_ref[step, lax.axis_index(COL)]
+    row = pairing_ref[step : step + 1, :]
+    mine = lax.broadcasted_iota(jnp.int32, row.shape, 1) == lax.axis_index(COL)
+    return jnp.max(jnp.where(mine, row, 0).astype(jnp.float32)).astype(jnp.int32)
 
 
 def load_blocks(refs, blocks):
-    for s in range(4):
-        blocks[s] = refs[0][:, s * WIDTH : (s + 1) * WIDTH] if len(refs) == 1 else refs[s][...]
+    if len(refs) == 1:
+        for s in range(4):
+            blocks[s] = refs[0][:, s * WIDTH : (s + 1) * WIDTH]
+    else:
+        low, high, near, far = refs
+        core = lax.axis_index(CORE)
+        blocks[0] = low[...]
+        blocks[2] = high[...]
+        blocks[3 - 2 * core] = near[1 - core]
+        blocks[1 + 2 * core] = far[...]
+
+
+def fetch_gram_kernel(pairing_hbm, slab_hbm, out, blocks, pairing, slab, sems):
+    copies = [
+        pltpu.make_async_copy(pairing_hbm, pairing, sems.at[0]),
+        pltpu.make_async_copy(slab_hbm, slab, sems.at[1]),
+    ]
+    for copy in copies:
+        copy.start()
+    for copy in copies:
+        copy.wait()
+    gram_kernel(0, pairing, slab, out, blocks)
 
 
 def gram_kernel(step, pairing_ref, *refs):
@@ -105,7 +128,14 @@
     for pair, (f, s) in enumerate(slots_of(pick(pairing_ref, step))):
         x = blocks[f]
         y = blocks[s]
-        cross = dot3(halves(x), halves(y), TN)
+        xh, xl = halves(x)
+        yh, yl = halves(y)
+        cross = lax.dot_general(
+            jnp.concatenate([xh, xh, xl], axis=0),
+            jnp.concatenate([yh, yl, yh], axis=0),
+            TN,
+            preferred_element_type=jnp.float32,
+        )
         for side, block in enumerate((x, y)):
             norm = jnp.sum(block * block, axis=0, keepdims=True)
             for h in range(2):
@@ -132,7 +162,7 @@
     pairs = slots_of(pick(pairing_ref, step))
     scale = lax.rsqrt(gram[0, NORMS:] + EPS)
     scale_t = scale.T
-    xs, ys, cs, ms, ts, starts, squares = [], [], [], [], [], [], []
+    xs, ys, cs, ms, ts, starts, m_squares = [], [], [], [], [], [], []
     bound = None
     for pair, (f, s) in enumerate(pairs):
         x = blocks[f]
@@ -145,22 +175,17 @@
             half = gram[:, start : start + PART, :].reshape(WIDTH, HALF)
             sides.append(half * down * scale[row + 2 + h : row + 3 + h])
         coupling[pair] = jnp.concatenate(sides, axis=1)
-        c = halves(coupling[pair])
-        both = dot3(stack(halves(y), c), c, NT)
-        t = x - both[:ROWS]
-        m = both[ROWS:]
-        mh = halves(m)
-        both = dot3(stack(halves(t), mh), mh, NN)
-        square = both[ROWS:]
-        most = jnp.sum(square * square)
-        bound = most if bound is None else jnp.maximum(bound, most)
+        cs.append(halves(coupling[pair]))
         xs.append(x)
         ys.append(y)
-        cs.append(c)
-        ms.append(m)
-        ts.append(t)
-        starts.append(both[:ROWS])
-        squares.append(square)
+    ms = dots3([(c, c) for c in cs], NT)
+    ts = [x - yc for x, yc in zip(xs, dots3([(halves(y), c) for y, c in zip(ys, cs)], NT))]
+    splits = [halves(m) for m in ms]
+    m_squares = dots3([(m, m) for m in splits], NN)
+    starts = dots3([(halves(t), m) for t, m in zip(ts, splits)], NN)
+    for pair in range(2):
+        most = jnp.sum(m_squares[pair] * m_squares[pair])
+        bound = most if bound is None else jnp.maximum(bound, most)
     b = jnp.sqrt(jnp.sqrt(jnp.full((8, 128), bound, jnp.float32)))[:1, :1] * 1.001
 
     @pl.when(bound <= SQUARINGS[-1][1])
@@ -171,25 +196,42 @@
             jnp.int32, (WIDTH, WIDTH), 1
         )
         for pair in range(2):
-            off = (relax * relax) * squares[pair] - (2.0 * keep * relax) * ms[pair]
+            off = (relax * relax) * m_squares[pair] - (2.0 * keep * relax) * ms[pair]
             powers[pair] = jnp.where(diagonal, off + keep * keep, off)
             solved[pair] = relax * ((1.0 + keep) * ts[pair] - relax * starts[pair])
 
         def body(_, carry):
+            zs = [solved[pair] for pair in range(2)]
+            rs = [halves(powers[pair]) for pair in range(2)]
+            zrs = dots3([(halves(z), r) for z, r in zip(zs, rs)], NN)
+            squares = dots3([(r, r) for r in rs], NN)
+            zs = [z + zr for z, zr in zip(zs, zrs)]
             for pair in range(2):
-                z = solved[pair]
-                r = halves(powers[pair])
-                both = dot3(stack(halves(z), r), r, NN)
-                solved[pair] = z + both[:ROWS]
-                powers[pair] = both[ROWS:]
+                solved[pair] = zs[pair]
+                powers[pair] = squares[pair]
             return carry
 
-        lax.fori_loop(0, count_of(bound, SQUARINGS), body, 0)
-        for pair, ((f, s), x, y, c) in enumerate(zip(pairs, xs, ys, cs)):
-            z = solved[pair]
-            z = z + dot3(halves(z), halves(powers[pair]), NN)
+        count = count_of(bound, SQUARINGS)
+        lax.fori_loop(1, count, body, 0)
+        top = keep
+        for index in range(len(SQUARINGS)):
+            top = jnp.where(count > index, top * top, top)
+        third = 1.0
+        second = third - 2.0 * top
+        first = second + 1.25 * top * top
+        zeroth = first - 0.25 * top * top * top
+        unit = 1.0 / (zeroth + top * top * top * top * (1.0 / 128.0))
+        zs = [solved[pair] for pair in range(2)]
+        rs = [halves(powers[pair]) for pair in range(2)]
+        squares = dots3([(r, r) for r in rs], NN)
+        zrs = dots3([(halves(z), r) for z, r in zip(zs, rs)], NN)
+        highs = [(unit * second) * z + unit * zr for z, zr in zip(zs, zrs)]
+        tops = dots3([(halves(h), halves(q)) for h, q in zip(highs, squares)], NN)
+        zs = [(unit * zeroth) * z + (unit * first) * zr + t for z, zr, t in zip(zs, zrs, tops)]
+        zcs = dots3([(halves(z), c) for z, c in zip(zs, cs)], NN)
+        for (f, s), x, y, z, zc in zip(pairs, xs, ys, zs, zcs):
             blocks[f] = 2.0 * z - x
-            blocks[s] = y + 2.0 * dot3(halves(z), c, NN)
+            blocks[s] = y + 2.0 * zc
 
     @pl.when(bound > SQUARINGS[-1][1])
     def _():
@@ -215,28 +257,50 @@
             blocks[f] = 2.0 * z - x
             blocks[s] = y + 2.0 * dot(z, c, NN)
 
-    for s in range(4):
-        if len(outs) == 1:
+    if len(outs) == 1:
+        for s in range(4):
             outs[0][:, s * WIDTH : (s + 1) * WIDTH] = blocks[s]
-        else:
-            outs[s][...] = blocks[s]
-
-
-SMEM = pl.BlockSpec(memory_space=pltpu.SMEM)
+    else:
+        low, high, near, far = outs
+        core = lax.axis_index(CORE)
+        low[...] = blocks[0]
+        high[...] = blocks[2]
+        near[0] = near[1] = blocks[1 + 2 * core]
+        far[...] = blocks[3 - 2 * core]
+
+
 VMEM = pl.BlockSpec(memory_space=pltpu.VMEM)
+HBM = pl.BlockSpec(memory_space=pltpu.HBM)
 BLOCKS = pltpu.VMEM((4, ROWS, WIDTH), jnp.float32)
 PARAMS = pltpu.CompilerParams(vmem_limit_bytes=8 * 2**20)
 
 
 def shape(*sizes):
     return jax.ShapeDtypeStruct(sizes, jnp.float32)
+
+
+def first_gram(pairing, slab):
+    return pl.pallas_call(
+        fetch_gram_kernel,
+        out_shape=shape(CHUNKS, NORMS + 8, HALF),
+        in_specs=[HBM] * 2,
+        out_specs=VMEM,
+        scratch_shapes=[
+            BLOCKS,
+            pltpu.VMEM(pairing.shape, pairing.dtype),
+            pltpu.VMEM(slab.shape, slab.dtype),
+            pltpu.SemaphoreType.DMA((2,)),
+        ],
+        compiler_params=PARAMS,
+        name="first_gram",
+    )(pairing, slab)
 
 
 def gram_of(step, pairing, ins):
     return pl.pallas_call(
         lambda *refs: gram_kernel(step, *refs),
         out_shape=shape(CHUNKS, NORMS + 8, HALF),
-        in_specs=[SMEM] + [VMEM] * len(ins),
+        in_specs=[VMEM] * (1 + len(ins)),
         out_specs=VMEM,
         scratch_shapes=[BLOCKS],
         compiler_params=PARAMS,
@@ -256,11 +320,11 @@
 
 
 def turn(step, pairing, gram, ins):
-    outs = [shape(ROWS, WIDTH)] * 4 if step == 0 else shape(ROWS, 4 * WIDTH)
+    outs = [shape(ROWS, WIDTH)] * 2 + [shape(2, ROWS, WIDTH), shape(ROWS, WIDTH)] if step == 0 else shape(ROWS, 4 * WIDTH)
     return pl.pallas_call(
         lambda *refs: turn_kernel(step, *refs),
         out_shape=outs,
-        in_specs=[SMEM] + [VMEM] * (1 + len(ins)),
+        in_specs=[VMEM] * (2 + len(ins)),
         out_specs=[VMEM] * 4 if step == 0 else VMEM,
         scratch_shapes=[
             BLOCKS,
@@ -281,11 +345,11 @@
 
 def local(slab, pairing):
     ins = (slab,)
-    gram = whole(gram_of(0, pairing, ins))
-    stay, ahead, wait, behind = turn(0, pairing, gram, ins)
-    ahead = lax.ppermute(ahead, COL, [(i, (i + 1) % 8) for i in range(8)])
-    behind = lax.ppermute(behind, COL, [(i, (i - 1) % 8) for i in range(8)])
-    ins = (stay, ahead, wait, behind)
+    gram = whole(first_gram(pairing, slab))
+    low, high, near, far = turn(0, pairing, gram, ins)
+    far = lax.ppermute(far, COL, [(i, (i + 1 if i % 2 else i - 1) % 8) for i in range(8)])
+    near = lax.all_to_all(near, CORE, 0, 0)
+    ins = (low, high, near, far)
     gram = whole(gram_of(1, pairing, ins))
     return turn(1, pairing, gram, ins)
 

time: 609 us -> 566 us (0.929)
  the two profiles are of different devices: /device:TPU:129 before, /device:TPU:8 now
where the time goes in v2:
time: 566 us
  Pallas kernels  470 us (83%)
  blocking collectives  88.5 us (16%)
    pallas_call x2, Pallas kernels, turn(): pl.pallas_call(lambda *refs: turn_kernel(step, *refs), out_shape=outs, in...  469 us
    all_to_all x2, blocking collectives, whole(): parts = add_up(lax.all_to_all(parts, OUTER, 0, 0), lax.axis_size(RING))  32.6 us
    all_to_all x2, blocking collectives, whole(): parts = add_up(lax.all_to_all(parts, RING, 0, 0), CHUNKS)  26.6 us
    all_to_all x2, blocking collectives, whole(): return lax.all_to_all(parts, OUTER, 0, 0)  25.4 us
  transfers between devices with their start and end apart: 1, of which 0 were waited for; matrix products, arithmetic and copies ran while one was open for 0% of the time, Pallas kernels for 0%

profile of v2, /device:TPU:8, one launch (start us, length us, event | category | flops | bytes accessed | tf_op | source)
XLA Modules:
  0.0 565.7 jit_solution(11451263802386048443)
XLA Ops:
  0.0 0.0 copy-start
  0.0 0.9 copy-done
  1.0 0.0 copy-start.2
  1.0 0.7 copy-done.2
  1.6 0.5 first_gram.1
  2.1 17.8 %all_to_all.35.parts = f32[16,72,128]{2,1,0:T(8,128)S(1)} all-to-all(f32[16,72,128]{2,1,0:T(8,128)S(1)} %first_gram.1), channel_id=1, replica_groups=mesh['z_lo'=2,'x'=4,'y_hi'=4,'y_lo'=2,'z_hi'=4,'core'=2] {'z_lo','x','y_..., dimensions={0} | all-to-all | bytes 1179648 | tf_op jit(solution)/shard_map/all_to_all | solution.py:341
  19.9 15.2 %all_to_all.36.parts = f32[4,72,128]{2,1,0:T(8,128)S(1)} all-to-all(f32[4,72,128]{2,1,0:T(8,128)S(1)} %add_up.4), channel_id=1, replica_groups=mesh['z_lo'=2,'x'=4,'y_hi'=4,'y_lo'=2,'z_hi'=4,'core'=2] {'y_hi'}, dimensions={0} | all-to-all | bytes 294912 | tf_op jit(solution)/shard_map/all_to_all | solution.py:342
  35.2 0.0 copy-start.1
  35.2 0.0 copy-start.3
  35.2 12.4 %all_to_all.37.refs_1_ = f32[16,72,128]{2,1,0:T(8,128)S(1)} all-to-all(f32[16,72,128]{2,1,0:T(8,128)S(1)} %add_up.5), channel_id=1, replica_groups=mesh['z_lo'=2,'x'=4,'y_hi'=4,'y_lo'=2,'z_hi'=4,'core'=2] {'z_lo','x','y_..., dimensions={0} | all-to-all | bytes 1179648 | tf_op jit(solution)/shard_map/all_to_all | solution.py:343
  47.6 0.0 copy-done.1
  47.6 0.0 copy-done.3
  47.6 183.6 %turn.2 = (f32[64,256]{1,0:T(8,128)S(1)}, f32[64,256]{1,0:T(8,128)S(1)}, f32[2,64,256]{2,1,0:T(8,128)S(1)}, f32[64,256]{1,0:T(8,128)S(1)}) custom-call(s32[2,8]{1,0:T(2,128)S(1)} %copy-done.3, f32[16,72,128]{2,1,0:T(8,128)S(1)} %all_to_all.37.refs_1_, f32[64,1024]{1,0:T(8,128)S(1)} %copy-done.1), custom_call_target="tpu_custom_call" | custom-call | tf_op jit(solution)/shard_map/turn/pallas_call | solution.py:324
  231.2 5.6 collective-permute-start
  236.9 3.9 all_to_all.38.refs_3_.refs_4_
  240.8 0.0 collective-permute-done.refs_4_.refs_5_
  240.8 0.4 gram.1
  241.2 14.9 %all_to_all.39.parts = f32[16,72,128]{2,1,0:T(8,128)S(1)} all-to-all(f32[16,72,128]{2,1,0:T(8,128)S(1)} %gram.1), channel_id=1, replica_groups=mesh['z_lo'=2,'x'=4,'y_hi'=4,'y_lo'=2,'z_hi'=4,'core'=2] {'z_lo','x','y_..., dimensions={0} | all-to-all | bytes 1179648 | tf_op jit(solution)/shard_map/all_to_all | solution.py:341
  256.1 11.3 %all_to_all.40.parts = f32[4,72,128]{2,1,0:T(8,128)S(1)} all-to-all(f32[4,72,128]{2,1,0:T(8,128)S(1)} %add_up.6), channel_id=1, replica_groups=mesh['z_lo'=2,'x'=4,'y_hi'=4,'y_lo'=2,'z_hi'=4,'core'=2] {'y_hi'}, dimensions={0} | all-to-all | bytes 294912 | tf_op jit(solution)/shard_map/all_to_all | solution.py:342
  267.4 13.0 %all_to_all.41.refs_1_ = f32[16,72,128]{2,1,0:T(8,128)S(1)} all-to-all(f32[16,72,128]{2,1,0:T(8,128)S(1)} %add_up.7), channel_id=1, replica_groups=mesh['z_lo'=2,'x'=4,'y_hi'=4,'y_lo'=2,'z_hi'=4,'core'=2] {'z_lo','x','y_..., dimensions={0} | all-to-all | bytes 1179648 | tf_op jit(solution)/shard_map/all_to_all | solution.py:343
  280.4 285.3 %turn.3 = f32[64,1024]{1,0:T(8,128)} custom-call(s32[2,8]{1,0:T(2,128)S(1)} %copy-done.3, f32[16,72,128]{2,1,0:T(8,128)S(1)} %all_to_all.41.refs_1_, f32[64,256]{1,0:T(8,128)S(1)} %get-tuple-element.9.refs_1_.refs_2_, f32[64,256]{1,0:T(8,128)S(1)} %get-tuple-element.10.refs_2_.refs_3_, f32[2,64,256]{2,1,0:T(8,128)S(1)} %all_to_all.38.refs_3_.refs_4_, ...), custom_call_target="tpu_custom_call" | custom-call | tf_op jit(solution)/shard_map/turn/pallas_call | solution.py:324
  (4 shorter events, 0.2 us)
Async XLA Ops:
  0.0 0.9 copy-start
  1.0 0.7 copy-start.2
  35.2 12.4 %copy-start.1 = (f32[64,1024]{1,0:T(8,128)S(1)}, f32[64,1024]{1,0:T(8,128)}, u32[]{:S(2)}) copy-start(f32[64,1024]{1,0:T(8,128)} %refs_2_.1) | copy-start | bytes 786436
  35.2 12.4 %copy-start.3 = (s32[2,8]{1,0:T(2,128)S(1)}, s32[2,8]{1,0:T(2,128)}, u32[]{:S(2)}) copy-start(s32[2,8]{1,0:T(2,128)} %refs_0_.5) | copy-start | bytes 196
  231.2 9.5 %collective-permute-start = (f32[64,256]{1,0:T(8,128)S(1)}, f32[64,256]{1,0:T(8,128)S(1)}, u32[]{:S(2)}, u32[]{:S(2)}) collective-permute-start(f32[64,256]{1,0:T(8,128)S(1)} %get-tuple-element.12), channel_id=1, source_target_pairs={{0,7},{1,2},{2,1},{3,4},{4,3},{5,6},{6,5},{7,0},{8,15},{9,10},{10,... | collective-permute-start | bytes 196616 | tf_op jit(solution)/shard_map/ppermute | solution.py:350

commit v3 on v2

--- a/solution.py
+++ b/solution.py
@@ -123,8 +123,7 @@
 def gram_kernel(step, pairing_ref, *refs):
     *ins, out, blocks = refs
     load_blocks(ins, blocks)
-    for c in range(1, CHUNKS):
-        out[c, NORMS:] = jnp.zeros((8, HALF), jnp.float32)
+    norms = []
     for pair, (f, s) in enumerate(slots_of(pick(pairing_ref, step))):
         x = blocks[f]
         y = blocks[s]
@@ -136,15 +135,16 @@
             TN,
             preferred_element_type=jnp.float32,
         )
-        for side, block in enumerate((x, y)):
+        for block in (x, y):
             norm = jnp.sum(block * block, axis=0, keepdims=True)
-            for h in range(2):
-                row = NORMS + 4 * pair + 2 * side + h
-                out[0, row : row + 1] = norm[:, h * HALF : (h + 1) * HALF]
+            norms += [norm[:, :HALF], norm[:, HALF:]]
         for h in range(2):
             start = (2 * pair + h) * PART
             half = cross[:, h * HALF : (h + 1) * HALF]
             out[:, start : start + PART, :] = half.reshape(CHUNKS, PART, HALF)
+    norms = jnp.concatenate(norms, axis=0)
+    for c in range(CHUNKS):
+        out[c, NORMS:] = norms
 
 
 def sum_kernel(parts, out):
@@ -155,25 +155,39 @@
         out[c] = total
 
 
+def couple_kernel(parts, out, down):
+    total = parts[0]
+    for c in range(1, parts.shape[0]):
+        total = total + parts[c]
+    across = lax.rsqrt(total[NORMS:] + EPS)
+    down[...] = across.T
+    chunk = lax.axis_index(OUTER)
+    half_chunks = CHUNKS // 2
+    rows = down[pl.ds(pl.multiple_of(lax.rem(chunk, half_chunks) * PART, PART), PART), :]
+    for pair in range(2):
+        row = 4 * pair
+        scale = jnp.where(chunk < half_chunks, rows[:, row : row + 1], rows[:, row + 1 : row + 2])
+        for h in range(2):
+            start = (2 * pair + h) * PART
+            part = total[start : start + PART] * scale * across[row + 2 + h : row + 3 + h]
+            for c in range(CHUNKS):
+                out[c, start : start + PART] = part
+
+
 def turn_kernel(step, pairing_ref, gram, *refs):
     count = 1 if step == 0 else 4
     ins, outs, (blocks, coupling, powers, solved) = refs[:count], refs[count:-4], refs[-4:]
     load_blocks(ins, blocks)
     pairs = slots_of(pick(pairing_ref, step))
-    scale = lax.rsqrt(gram[0, NORMS:] + EPS)
-    scale_t = scale.T
     xs, ys, cs, ms, ts, starts, m_squares = [], [], [], [], [], [], []
     bound = None
     for pair, (f, s) in enumerate(pairs):
         x = blocks[f]
         y = blocks[s]
-        row = 4 * pair
-        down = jnp.concatenate([scale_t[:, row : row + 1], scale_t[:, row + 1 : row + 2]], axis=0)
         sides = []
         for h in range(2):
             start = (2 * pair + h) * PART
-            half = gram[:, start : start + PART, :].reshape(WIDTH, HALF)
-            sides.append(half * down * scale[row + 2 + h : row + 3 + h])
+            sides.append(gram[:, start : start + PART, :].reshape(WIDTH, HALF))
         coupling[pair] = jnp.concatenate(sides, axis=1)
         cs.append(halves(coupling[pair]))
         xs.append(x)
@@ -319,6 +333,18 @@
     )(parts)
 
 
+def couple(parts):
+    return pl.pallas_call(
+        couple_kernel,
+        out_shape=shape(CHUNKS, NORMS, HALF),
+        in_specs=[VMEM],
+        out_specs=VMEM,
+        scratch_shapes=[pltpu.VMEM((HALF, 8), jnp.float32)],
+        compiler_params=PARAMS,
+        name="couple",
+    )(parts)
+
+
 def turn(step, pairing, gram, ins):
     outs = [shape(ROWS, WIDTH)] * 2 + [shape(2, ROWS, WIDTH), shape(ROWS, WIDTH)] if step == 0 else shape(ROWS, 4 * WIDTH)
     return pl.pallas_call(
@@ -339,13 +365,13 @@
 
 def whole(parts):
     parts = add_up(lax.all_to_all(parts, OUTER, 0, 0), lax.axis_size(RING))
-    parts = add_up(lax.all_to_all(parts, RING, 0, 0), CHUNKS)
+    parts = couple(lax.all_to_all(parts, RING, 0, 0))
     return lax.all_to_all(parts, OUTER, 0, 0)
 
 
 def local(slab, pairing):
     ins = (slab,)
-    gram = whole(first_gram(pairing, slab))
+    gram = whole(first_gram(pltpu.with_memory_space_constraint(pairing, pltpu.HBM), pltpu.with_memory_space_constraint(slab, pltpu.HBM)))
     low, high, near, far = turn(0, pairing, gram, ins)
     far = lax.ppermute(far, COL, [(i, (i + 1 if i % 2 else i - 1) % 8) for i in range(8)])
     near = lax.all_to_all(near, CORE, 0, 0)

time: 566 us -> 565 us (level)
  the two profiles are of different devices: /device:TPU:8 before, /device:TPU:128 now
where the time goes in v3:
time: 565 us; the launch traced here: 564 us
  Pallas kernels  471 us (83%)
  blocking collectives  91.6 us (16%)
    pallas_call x2, Pallas kernels, turn(): pl.pallas_call(lambda *refs: turn_kernel(step, *refs), out_shape=outs, in...  468 us
    all_to_all x2, blocking collectives, whole(): parts = add_up(lax.all_to_all(parts, OUTER, 0, 0), lax.axis_size(RING))  34.4 us
    all_to_all x2, blocking collectives, whole(): parts = couple(lax.all_to_all(parts, RING, 0, 0))  26.1 us
    all_to_all x2, blocking collectives, whole(): return lax.all_to_all(parts, OUTER, 0, 0)  23.1 us
  transfers between devices with their start and end apart: 1, of which 0 were waited for; matrix products, arithmetic and copies ran while one was open for 0% of the time, Pallas kernels for 0%

profile of v3, /device:TPU:128, one launch (start us, length us, event | category | flops | bytes accessed | tf_op | source)
XLA Modules:
  0.0 564.3 jit_solution(13603011628178010739)
XLA Ops:
  0.0 1.4 first_gram.1
  1.4 18.7 %all_to_all.35.parts = f32[16,72,128]{2,1,0:T(8,128)S(1)} all-to-all(f32[16,72,128]{2,1,0:T(8,128)S(1)} %first_gram.1), channel_id=1, replica_groups=mesh['z_lo'=2,'x'=4,'y_hi'=4,'y_lo'=2,'z_hi'=4,'core'=2] {'z_lo','x','y_..., dimensions={0} | all-to-all | bytes 1179648 | tf_op jit(solution)/shard_map/all_to_all | solution.py:367
  20.1 14.9 %all_to_all.36.parts = f32[4,72,128]{2,1,0:T(8,128)S(1)} all-to-all(f32[4,72,128]{2,1,0:T(8,128)S(1)} %add_up.2), channel_id=1, replica_groups=mesh['z_lo'=2,'x'=4,'y_hi'=4,'y_lo'=2,'z_hi'=4,'core'=2] {'y_hi'}, dimensions={0} | all-to-all | bytes 294912 | tf_op jit(solution)/shard_map/all_to_all | solution.py:368
  35.0 0.3 couple.2
  35.3 0.0 copy-start
  35.3 0.0 copy-start.1
  35.3 11.5 %all_to_all.37.refs_1_ = f32[16,64,128]{2,1,0:T(8,128)S(1)} all-to-all(f32[16,64,128]{2,1,0:T(8,128)S(1)} %couple.2), channel_id=1, replica_groups=mesh['z_lo'=2,'x'=4,'y_hi'=4,'y_lo'=2,'z_hi'=4,'core'=2] {'z_lo','x','y_..., dimensions={0} | all-to-all | bytes 1048576 | tf_op jit(solution)/shard_map/all_to_all | solution.py:369
  46.8 0.0 copy-done
  46.8 0.0 copy-done.1
  46.8 183.2 %turn.2 = (f32[64,256]{1,0:T(8,128)S(1)}, f32[64,256]{1,0:T(8,128)S(1)}, f32[2,64,256]{2,1,0:T(8,128)S(1)}, f32[64,256]{1,0:T(8,128)S(1)}) custom-call(s32[2,8]{1,0:T(2,128)S(1)} %copy-done.1, f32[16,64,128]{2,1,0:T(8,128)S(1)} %all_to_all.37.refs_1_, f32[64,1024]{1,0:T(8,128)S(1)} %copy-done), custom_call_target="tpu_custom_call" | custom-call | tf_op jit(solution)/shard_map/turn/pallas_call | solution.py:350
  230.0 1.9 collective-permute-start
  231.9 7.9 %all_to_all.38.refs_3_.refs_4_ = f32[2,64,256]{2,1,0:T(8,128)S(1)} all-to-all(f32[2,64,256]{2,1,0:T(8,128)S(1)} %get-tuple-element.11), channel_id=1, replica_groups=mesh['z_lo'=2,'x'=4,'y_hi'=4,'y_lo'=2,'z_hi'=4,'core'=2] {'core'}, dimensions={0} | all-to-all | bytes 262144 | tf_op jit(solution)/shard_map/all_to_all | solution.py:377
  239.9 0.0 collective-permute-done.refs_4_.refs_5_
  239.9 0.4 gram.1
  240.3 15.7 %all_to_all.39.parts = f32[16,72,128]{2,1,0:T(8,128)S(1)} all-to-all(f32[16,72,128]{2,1,0:T(8,128)S(1)} %gram.1), channel_id=1, replica_groups=mesh['z_lo'=2,'x'=4,'y_hi'=4,'y_lo'=2,'z_hi'=4,'core'=2] {'z_lo','x','y_..., dimensions={0} | all-to-all | bytes 1179648 | tf_op jit(solution)/shard_map/all_to_all | solution.py:367
  256.1 11.3 %all_to_all.40.parts = f32[4,72,128]{2,1,0:T(8,128)S(1)} all-to-all(f32[4,72,128]{2,1,0:T(8,128)S(1)} %add_up.3), channel_id=1, replica_groups=mesh['z_lo'=2,'x'=4,'y_hi'=4,'y_lo'=2,'z_hi'=4,'core'=2] {'y_hi'}, dimensions={0} | all-to-all | bytes 294912 | tf_op jit(solution)/shard_map/all_to_all | solution.py:368
  267.3 0.3 couple.3
  267.6 11.6 %all_to_all.41.refs_1_ = f32[16,64,128]{2,1,0:T(8,128)S(1)} all-to-all(f32[16,64,128]{2,1,0:T(8,128)S(1)} %couple.3), channel_id=1, replica_groups=mesh['z_lo'=2,'x'=4,'y_hi'=4,'y_lo'=2,'z_hi'=4,'core'=2] {'z_lo','x','y_..., dimensions={0} | all-to-all | bytes 1048576 | tf_op jit(solution)/shard_map/all_to_all | solution.py:369
  279.2 285.1 %turn.3 = f32[64,1024]{1,0:T(8,128)} custom-call(s32[2,8]{1,0:T(2,128)S(1)} %copy-done.1, f32[16,64,128]{2,1,0:T(8,128)S(1)} %all_to_all.41.refs_1_, f32[64,256]{1,0:T(8,128)S(1)} %get-tuple-element.9.refs_1_.refs_2_, f32[64,256]{1,0:T(8,128)S(1)} %get-tuple-element.10.refs_2_.refs_3_, f32[2,64,256]{2,1,0:T(8,128)S(1)} %all_to_all.38.refs_3_.refs_4_, ...), custom_call_target="tpu_custom_call" | custom-call | tf_op jit(solution)/shard_map/turn/pallas_call | solution.py:350
  (2 shorter events, 0.1 us)
Async XLA Ops:
  35.3 11.5 %copy-start = (f32[64,1024]{1,0:T(8,128)S(1)}, f32[64,1024]{1,0:T(8,128)}, u32[]{:S(2)}) copy-start(f32[64,1024]{1,0:T(8,128)} %refs_2_.1) | copy-start | bytes 786436
  35.3 11.5 %copy-start.1 = (s32[2,8]{1,0:T(2,128)S(1)}, s32[2,8]{1,0:T(2,128)}, u32[]{:S(2)}) copy-start(s32[2,8]{1,0:T(2,128)} %refs_0_.5) | copy-start | bytes 196
  230.0 9.9 %collective-permute-start = (f32[64,256]{1,0:T(8,128)S(1)}, f32[64,256]{1,0:T(8,128)S(1)}, u32[]{:S(2)}, u32[]{:S(2)}) collective-permute-start(f32[64,256]{1,0:T(8,128)S(1)} %get-tuple-element.12), channel_id=1, source_target_pairs={{0,7},{1,2},{2,1},{3,4},{4,3},{5,6},{6,5},{7,0},{8,15},{9,10},{10,... | collective-permute-start | bytes 196616 | tf_op jit(solution)/shard_map/ppermute | solution.py:376

commit v4 on v3

--- a/solution.py
+++ b/solution.py
@@ -13,8 +13,10 @@
 HALF = 128
 ROWS = 64
 CHUNKS = 16
-PART = WIDTH // CHUNKS
-NORMS = 4 * PART
+PART = 32
+BANDS = WIDTH // PART
+NORMS = 2 * PART
+FULL = NORMS + 4
 OUTER = ("z_lo", "x", "y_lo")
 RING = ("y_hi",)
 COL = ("z_hi", "core")
@@ -26,7 +28,7 @@
 
 
 TOLERANCE = 2e-6
-CUBIC_TOLERANCE = 1e-5
+CLOSING_TOLERANCE = 1e-5
 
 
 def step_table():
@@ -45,12 +47,15 @@
     return fourth(table)
 
 
-def squaring_table():
-    rho = (0.5 * CUBIC_TOLERANCE) ** 0.25
-    top = 4.0 * rho / (1.0 + rho) ** 2
+def widest(degree):
+    rho = (0.5 * CLOSING_TOLERANCE) ** (1.0 / (degree + 1))
+    return 4.0 * rho / (1.0 + rho) ** 2
+
+
+def squaring_table(degree):
     table = []
-    for count in range(1, 7):
-        mu = top ** (0.5**count)
+    for count in range(1, 6):
+        mu = widest(degree) ** (0.5**count)
         table.append((count, 2.0 * mu / (1.0 - mu)))
     return fourth(table)
 
@@ -67,7 +72,8 @@
 
 
 STEPS = step_table()
-SQUARINGS = squaring_table()
+CUBIC = squaring_table(3)[0][1]
+SQUARINGS = squaring_table(5)
 
 
 def halves(a):
@@ -135,16 +141,18 @@
             TN,
             preferred_element_type=jnp.float32,
         )
-        for block in (x, y):
-            norm = jnp.sum(block * block, axis=0, keepdims=True)
-            norms += [norm[:, :HALF], norm[:, HALF:]]
+        norms.append([jnp.sum(block * block, axis=0, keepdims=True) for block in (x, y)])
         for h in range(2):
-            start = (2 * pair + h) * PART
-            half = cross[:, h * HALF : (h + 1) * HALF]
-            out[:, start : start + PART, :] = half.reshape(CHUNKS, PART, HALF)
-    norms = jnp.concatenate(norms, axis=0)
-    for c in range(CHUNKS):
-        out[c, NORMS:] = norms
+            half = cross[:, h * HALF : (h + 1) * HALF].reshape(BANDS, PART, HALF)
+            out[h * BANDS : (h + 1) * BANDS, pair * PART : (pair + 1) * PART, :] = half
+    (xa, ya), (xb, yb) = norms
+    for h in range(2):
+        for g in range(2):
+            columns = slice(h * HALF, (h + 1) * HALF)
+            rows = slice(g * HALF, (g + 1) * HALF)
+            tail = jnp.concatenate([ya[:, columns], yb[:, columns], xa[:, rows], xb[:, rows]], axis=0)
+            for k in range(BANDS // 2):
+                out[h * BANDS + g * (BANDS // 2) + k, NORMS:] = tail
 
 
 def sum_kernel(parts, out):
@@ -160,18 +168,14 @@
     for c in range(1, parts.shape[0]):
         total = total + parts[c]
     across = lax.rsqrt(total[NORMS:] + EPS)
-    down[...] = across.T
-    chunk = lax.axis_index(OUTER)
-    half_chunks = CHUNKS // 2
-    rows = down[pl.ds(pl.multiple_of(lax.rem(chunk, half_chunks) * PART, PART), PART), :]
+    down[...] = jnp.concatenate([across, across], axis=0).T
+    start = pl.multiple_of(lax.rem(lax.axis_index(OUTER), HALF // PART) * PART, PART)
+    rows = down[pl.ds(start, PART), :]
     for pair in range(2):
-        row = 4 * pair
-        scale = jnp.where(chunk < half_chunks, rows[:, row : row + 1], rows[:, row + 1 : row + 2])
-        for h in range(2):
-            start = (2 * pair + h) * PART
-            part = total[start : start + PART] * scale * across[row + 2 + h : row + 3 + h]
-            for c in range(CHUNKS):
-                out[c, start : start + PART] = part
+        part = total[pair * PART : (pair + 1) * PART]
+        part = part * rows[:, 2 + pair : 3 + pair] * across[pair : pair + 1]
+        for c in range(CHUNKS):
+            out[c, pair * PART : (pair + 1) * PART] = part
 
 
 def turn_kernel(step, pairing_ref, gram, *refs):
@@ -186,8 +190,8 @@
         y = blocks[s]
         sides = []
         for h in range(2):
-            start = (2 * pair + h) * PART
-            sides.append(gram[:, start : start + PART, :].reshape(WIDTH, HALF))
+            part = gram[h * BANDS : (h + 1) * BANDS, pair * PART : (pair + 1) * PART, :]
+            sides.append(part.reshape(WIDTH, HALF))
         coupling[pair] = jnp.concatenate(sides, axis=1)
         cs.append(halves(coupling[pair]))
         xs.append(x)
@@ -230,17 +234,33 @@
         top = keep
         for index in range(len(SQUARINGS)):
             top = jnp.where(count > index, top * top, top)
-        third = 1.0
-        second = third - 2.0 * top
-        first = second + 1.25 * top * top
-        zeroth = first - 0.25 * top * top * top
-        unit = 1.0 / (zeroth + top * top * top * top * (1.0 / 128.0))
+        cubic = bound <= CUBIC
+        top2 = top * top
+        top3 = top2 * top
+        top4 = top2 * top2
+        zero = jnp.zeros_like(top)
+        fifth = jnp.where(cubic, zero, zero + 1.0)
+        fourth = jnp.where(cubic, zero, 1.0 - 3.0 * top)
+        third = jnp.where(cubic, zero + 1.0, fourth + 3.375 * top2)
+        second = third - jnp.where(cubic, 2.0 * top, 1.75 * top3)
+        first = second + jnp.where(cubic, 1.25 * top2, 0.41015625 * top4)
+        zeroth = first - jnp.where(cubic, 0.25 * top3, 0.03515625 * top4 * top)
+        unit = 1.0 / (zeroth + jnp.where(cubic, top4 * (1.0 / 128.0), top4 * top2 * (1.0 / 2048.0)))
         zs = [solved[pair] for pair in range(2)]
         rs = [halves(powers[pair]) for pair in range(2)]
-        squares = dots3([(r, r) for r in rs], NN)
+        squares = [halves(q) for q in dots3([(r, r) for r in rs], NN)]
         zrs = dots3([(halves(z), r) for z, r in zip(zs, rs)], NN)
-        highs = [(unit * second) * z + unit * zr for z, zr in zip(zs, zrs)]
-        tops = dots3([(halves(h), halves(q)) for h, q in zip(highs, squares)], NN)
+        for pair in range(2):
+            solved[pair] = (unit * second) * zs[pair] + (unit * third) * zrs[pair]
+
+        @pl.when(jnp.logical_not(cubic))
+        def _():
+            highs = [(unit * fourth) * z + (unit * fifth) * zr for z, zr in zip(zs, zrs)]
+            tops = dots3([(halves(h), q) for h, q in zip(highs, squares)], NN)
+            for pair in range(2):
+                solved[pair] += tops[pair]
+
+        tops = dots3([(halves(solved[pair]), squares[pair]) for pair in range(2)], NN)
         zs = [(unit * zeroth) * z + (unit * first) * zr + t for z, zr, t in zip(zs, zrs, tops)]
         zcs = dots3([(halves(z), c) for z, c in zip(zs, cs)], NN)
         for (f, s), x, y, z, zc in zip(pairs, xs, ys, zs, zcs):
@@ -296,7 +316,7 @@
 def first_gram(pairing, slab):
     return pl.pallas_call(
         fetch_gram_kernel,
-        out_shape=shape(CHUNKS, NORMS + 8, HALF),
+        out_shape=shape(CHUNKS, FULL, HALF),
         in_specs=[HBM] * 2,
         out_specs=VMEM,
         scratch_shapes=[
@@ -313,7 +333,7 @@
 def gram_of(step, pairing, ins):
     return pl.pallas_call(
         lambda *refs: gram_kernel(step, *refs),
-        out_shape=shape(CHUNKS, NORMS + 8, HALF),
+        out_shape=shape(CHUNKS, FULL, HALF),
         in_specs=[VMEM] * (1 + len(ins)),
         out_specs=VMEM,
         scratch_shapes=[BLOCKS],

time: 565 us -> 565 us (level)
  no operation moved by 1% of the time
where the time goes in v4:
time: 565 us; the launch traced here: 564 us
  Pallas kernels  471 us (83%)
  blocking collectives  91.6 us (16%)
    pallas_call x2, Pallas kernels, turn(): pl.pallas_call(lambda *refs: turn_kernel(step, *refs), out_shape=outs, in...  468 us
    all_to_all x2, blocking collectives, whole(): parts = add_up(lax.all_to_all(parts, OUTER, 0, 0), lax.axis_size(RING))  34.4 us
    all_to_all x2, blocking collectives, whole(): parts = couple(lax.all_to_all(parts, RING, 0, 0))  26.1 us
    all_to_all x2, blocking collectives, whole(): return lax.all_to_all(parts, OUTER, 0, 0)  23.1 us
  transfers between devices with their start and end apart: 1, of which 0 were waited for; matrix products, arithmetic and copies ran while one was open for 0% of the time, Pallas kernels for 0%

profile of v4, /device:TPU:128, one launch (start us, length us, event | category | flops | bytes accessed | tf_op | source)
XLA Modules:
  0.0 564.4 jit_solution(2642545811672235929)
XLA Ops:
  0.0 1.4 first_gram.1
  1.4 18.7 %all_to_all.35.parts = f32[16,68,128]{2,1,0:T(8,128)S(1)} all-to-all(f32[16,68,128]{2,1,0:T(8,128)S(1)} %first_gram.1), channel_id=1, replica_groups=mesh['z_lo'=2,'x'=4,'y_hi'=4,'y_lo'=2,'z_hi'=4,'core'=2] {'z_lo','x','y_..., dimensions={0} | all-to-all | bytes 1114112 | tf_op jit(solution)/shard_map/all_to_all | solution.py:387
  20.1 14.9 %all_to_all.36.parts = f32[4,68,128]{2,1,0:T(8,128)S(1)} all-to-all(f32[4,68,128]{2,1,0:T(8,128)S(1)} %add_up.2), channel_id=1, replica_groups=mesh['z_lo'=2,'x'=4,'y_hi'=4,'y_lo'=2,'z_hi'=4,'core'=2] {'y_hi'}, dimensions={0} | all-to-all | bytes 278528 | tf_op jit(solution)/shard_map/all_to_all | solution.py:388
  35.0 0.2 couple.2
  35.2 0.0 copy-start
  35.2 0.0 copy-start.1
  35.3 11.5 %all_to_all.37.refs_1_ = f32[16,64,128]{2,1,0:T(8,128)S(1)} all-to-all(f32[16,64,128]{2,1,0:T(8,128)S(1)} %couple.2), channel_id=1, replica_groups=mesh['z_lo'=2,'x'=4,'y_hi'=4,'y_lo'=2,'z_hi'=4,'core'=2] {'z_lo','x','y_..., dimensions={0} | all-to-all | bytes 1048576 | tf_op jit(solution)/shard_map/all_to_all | solution.py:389
  46.8 0.0 copy-done
  46.8 0.0 copy-done.1
  46.8 183.4 %turn.2 = (f32[64,256]{1,0:T(8,128)S(1)}, f32[64,256]{1,0:T(8,128)S(1)}, f32[2,64,256]{2,1,0:T(8,128)S(1)}, f32[64,256]{1,0:T(8,128)S(1)}) custom-call(s32[2,8]{1,0:T(2,128)S(1)} %copy-done.1, f32[16,64,128]{2,1,0:T(8,128)S(1)} %all_to_all.37.refs_1_, f32[64,1024]{1,0:T(8,128)S(1)} %copy-done), custom_call_target="tpu_custom_call" | custom-call | tf_op jit(solution)/shard_map/turn/pallas_call | solution.py:370
  230.1 1.9 collective-permute-start
  232.1 7.9 %all_to_all.38.refs_3_.refs_4_ = f32[2,64,256]{2,1,0:T(8,128)S(1)} all-to-all(f32[2,64,256]{2,1,0:T(8,128)S(1)} %get-tuple-element.11), channel_id=1, replica_groups=mesh['z_lo'=2,'x'=4,'y_hi'=4,'y_lo'=2,'z_hi'=4,'core'=2] {'core'}, dimensions={0} | all-to-all | bytes 262144 | tf_op jit(solution)/shard_map/all_to_all | solution.py:397
  240.0 0.0 collective-permute-done.refs_4_.refs_5_
  240.0 0.4 gram.1
  240.4 15.7 %all_to_all.39.parts = f32[16,68,128]{2,1,0:T(8,128)S(1)} all-to-all(f32[16,68,128]{2,1,0:T(8,128)S(1)} %gram.1), channel_id=1, replica_groups=mesh['z_lo'=2,'x'=4,'y_hi'=4,'y_lo'=2,'z_hi'=4,'core'=2] {'z_lo','x','y_..., dimensions={0} | all-to-all | bytes 1114112 | tf_op jit(solution)/shard_map/all_to_all | solution.py:387
  256.2 11.3 %all_to_all.40.parts = f32[4,68,128]{2,1,0:T(8,128)S(1)} all-to-all(f32[4,68,128]{2,1,0:T(8,128)S(1)} %add_up.3), channel_id=1, replica_groups=mesh['z_lo'=2,'x'=4,'y_hi'=4,'y_lo'=2,'z_hi'=4,'core'=2] {'y_hi'}, dimensions={0} | all-to-all | bytes 278528 | tf_op jit(solution)/shard_map/all_to_all | solution.py:388
  267.5 0.2 couple.3
  267.7 11.6 %all_to_all.41.refs_1_ = f32[16,64,128]{2,1,0:T(8,128)S(1)} all-to-all(f32[16,64,128]{2,1,0:T(8,128)S(1)} %couple.3), channel_id=1, replica_groups=mesh['z_lo'=2,'x'=4,'y_hi'=4,'y_lo'=2,'z_hi'=4,'core'=2] {'z_lo','x','y_..., dimensions={0} | all-to-all | bytes 1048576 | tf_op jit(solution)/shard_map/all_to_all | solution.py:389
  279.3 285.1 %turn.3 = f32[64,1024]{1,0:T(8,128)} custom-call(s32[2,8]{1,0:T(2,128)S(1)} %copy-done.1, f32[16,64,128]{2,1,0:T(8,128)S(1)} %all_to_all.41.refs_1_, f32[64,256]{1,0:T(8,128)S(1)} %get-tuple-element.9.refs_1_.refs_2_, f32[64,256]{1,0:T(8,128)S(1)} %get-tuple-element.10.refs_2_.refs_3_, f32[2,64,256]{2,1,0:T(8,128)S(1)} %all_to_all.38.refs_3_.refs_4_, ...), custom_call_target="tpu_custom_call" | custom-call | tf_op jit(solution)/shard_map/turn/pallas_call | solution.py:370
  (2 shorter events, 0.1 us)
Async XLA Ops:
  35.2 11.5 %copy-start = (f32[64,1024]{1,0:T(8,128)S(1)}, f32[64,1024]{1,0:T(8,128)}, u32[]{:S(2)}) copy-start(f32[64,1024]{1,0:T(8,128)} %refs_2_.1) | copy-start | bytes 786436
  35.2 11.5 %copy-start.1 = (s32[2,8]{1,0:T(2,128)S(1)}, s32[2,8]{1,0:T(2,128)}, u32[]{:S(2)}) copy-start(s32[2,8]{1,0:T(2,128)} %refs_0_.5) | copy-start | bytes 196
  230.1 9.9 %collective-permute-start = (f32[64,256]{1,0:T(8,128)S(1)}, f32[64,256]{1,0:T(8,128)S(1)}, u32[]{:S(2)}, u32[]{:S(2)}) collective-permute-start(f32[64,256]{1,0:T(8,128)S(1)} %get-tuple-element.12), channel_id=1, source_target_pairs={{0,7},{1,2},{2,1},{3,4},{4,3},{5,6},{6,5},{7,0},{8,15},{9,10},{10,... | collective-permute-start | bytes 196616 | tf_op jit(solution)/shard_map/ppermute | solution.py:396

commit v5 on v4

--- a/solution.py
+++ b/solution.py
@@ -83,10 +83,23 @@
 
 def dots3(operands, dims):
     dot = lambda u, v: lax.dot_general(u, v, dims, preferred_element_type=jnp.float32)
-    tops = [dot(a[0], b[0]) for a, b in operands]
+    rows = [a[0].shape[0] for a, _ in operands]
+    both = [dot(jnp.concatenate(a, axis=0), b[0]) for a, b in operands]
     lows = [dot(a[0], b[1]) for a, b in operands]
-    highs = [dot(a[1], b[0]) for a, b in operands]
-    return [t + (l + h) for t, l, h in zip(tops, lows, highs)]
+    return [t[:r] + (l + t[r:]) for t, l, r in zip(both, lows, rows)]
+
+
+def shared3(lefts, rights, dims):
+    joined = [tuple(jnp.concatenate(p, axis=0) for p in zip(*ls)) for ls in lefts]
+    products = dots3(list(zip(joined, rights)), dims)
+    out = []
+    for ls, product in zip(lefts, products):
+        start, parts = 0, []
+        for l in ls:
+            parts.append(product[start : start + l[0].shape[0]])
+            start += l[0].shape[0]
+        out.append(parts)
+    return out
 
 
 def slots_of(which):
@@ -143,8 +156,9 @@
         )
         norms.append([jnp.sum(block * block, axis=0, keepdims=True) for block in (x, y)])
         for h in range(2):
-            half = cross[:, h * HALF : (h + 1) * HALF].reshape(BANDS, PART, HALF)
-            out[h * BANDS : (h + 1) * BANDS, pair * PART : (pair + 1) * PART, :] = half
+            for k in range(BANDS):
+                start = (h * BANDS + k) * FULL + pair * PART
+                out[start : start + PART, :] = cross[k * PART : (k + 1) * PART, h * HALF : (h + 1) * HALF]
     (xa, ya), (xb, yb) = norms
     for h in range(2):
         for g in range(2):
@@ -152,21 +166,25 @@
             rows = slice(g * HALF, (g + 1) * HALF)
             tail = jnp.concatenate([ya[:, columns], yb[:, columns], xa[:, rows], xb[:, rows]], axis=0)
             for k in range(BANDS // 2):
-                out[h * BANDS + g * (BANDS // 2) + k, NORMS:] = tail
+                start = (h * BANDS + g * (BANDS // 2) + k) * FULL + NORMS
+                out[start : start + FULL - NORMS, :] = tail
+
+
+def total_of(parts):
+    total = parts[:FULL]
+    for start in range(FULL, parts.shape[0], FULL):
+        total = total + parts[start : start + FULL]
+    return total
 
 
 def sum_kernel(parts, out):
-    total = parts[0]
-    for c in range(1, parts.shape[0]):
-        total = total + parts[c]
-    for c in range(out.shape[0]):
-        out[c] = total
+    total = total_of(parts)
+    for start in range(0, out.shape[0], FULL):
+        out[start : start + FULL] = total
 
 
 def couple_kernel(parts, out, down):
-    total = parts[0]
-    for c in range(1, parts.shape[0]):
-        total = total + parts[c]
+    total = total_of(parts)
     across = lax.rsqrt(total[NORMS:] + EPS)
     down[...] = jnp.concatenate([across, across], axis=0).T
     start = pl.multiple_of(lax.rem(lax.axis_index(OUTER), HALF // PART) * PART, PART)
@@ -316,7 +334,7 @@
 def first_gram(pairing, slab):
     return pl.pallas_call(
         fetch_gram_kernel,
-        out_shape=shape(CHUNKS, FULL, HALF),
+        out_shape=shape(CHUNKS * FULL, HALF),
         in_specs=[HBM] * 2,
         out_specs=VMEM,
         scratch_shapes=[
@@ -333,7 +351,7 @@
 def gram_of(step, pairing, ins):
     return pl.pallas_call(
         lambda *refs: gram_kernel(step, *refs),
-        out_shape=shape(CHUNKS, FULL, HALF),
+        out_shape=shape(CHUNKS * FULL, HALF),
         in_specs=[VMEM] * (1 + len(ins)),
         out_specs=VMEM,
         scratch_shapes=[BLOCKS],
@@ -345,7 +363,7 @@
 def add_up(parts, copies):
     return pl.pallas_call(
         sum_kernel,
-        out_shape=shape(copies, *parts.shape[1:]),
+        out_shape=shape(copies * FULL, HALF),
         in_specs=[VMEM],
         out_specs=VMEM,
         compiler_params=PARAMS,
@@ -383,10 +401,15 @@
     )(pairing, gram, *ins)
 
 
+def exchange(parts, axes):
+    count = lax.axis_size(axes)
+    parts = lax.all_to_all(parts.reshape(count, FULL // 4, 4, HALF), axes, 0, 0)
+    return parts.reshape(count * FULL, HALF)
+
+
 def whole(parts):
-    parts = add_up(lax.all_to_all(parts, OUTER, 0, 0), lax.axis_size(RING))
-    parts = couple(lax.all_to_all(parts, RING, 0, 0))
-    return lax.all_to_all(parts, OUTER, 0, 0)
+    parts = add_up(exchange(parts, OUTER), lax.axis_size(RING))
+    return lax.all_to_all(couple(exchange(parts, RING)), OUTER, 0, 0)
 
 
 def local(slab, pairing):

time: 565 us -> 564 us (level)
  the two profiles are of different devices: /device:TPU:128 before, /device:TPU:8 now
where the time goes in v5:
time: 564 us; the launch traced here: 563 us
  Pallas kernels  471 us (84%)
  blocking collectives  86.9 us (15%)
    pallas_call x2, Pallas kernels, turn(): pl.pallas_call(lambda *refs: turn_kernel(step, *refs), out_shape=outs, in...  468 us
    all_to_all x4, blocking collectives, exchange(): parts = lax.all_to_all(parts.reshape(count, FULL // 4, 4, HALF), axes, 0, 0)  58.3 us
    all_to_all x2, blocking collectives, whole(): return lax.all_to_all(couple(exchange(parts, RING)), OUTER, 0, 0)  24.6 us
  transfers between devices with their start and end apart: 1, of which 0 were waited for; matrix products, arithmetic and copies ran while one was open for 0% of the time, Pallas kernels for 0%

profile of v5, /device:TPU:8, one launch (start us, length us, event | category | flops | bytes accessed | tf_op | source)
XLA Modules:
  0.0 563.1 jit_solution(3283620259835188105)
XLA Ops:
  0.0 1.4 first_gram.1
  1.4 17.5 %all_to_all.35 = f32[16,17,4,128]{3,2,1,0:T(4,128)S(1)} all-to-all(f32[16,17,4,128]{3,2,1,0:T(4,128)S(1)} %bitcast.10), channel_id=1, replica_groups=mesh['z_lo'=2,'x'=4,'y_hi'=4,'y_lo'=2,'z_hi'=4,'core'=2] {'z_lo','x','y_..., dimensions={0} | all-to-all | bytes 1114112 | tf_op jit(solution)/shard_map/all_to_all | solution.py:406
  19.0 15.1 %all_to_all.36 = f32[4,17,4,128]{3,2,1,0:T(4,128)S(1)} all-to-all(f32[4,17,4,128]{3,2,1,0:T(4,128)S(1)} %bitcast.12), channel_id=1, replica_groups=mesh['z_lo'=2,'x'=4,'y_hi'=4,'y_lo'=2,'z_hi'=4,'core'=2] {'y_hi'}, dimensions={0} | all-to-all | bytes 278528 | tf_op jit(solution)/shard_map/all_to_all | solution.py:406
  34.1 0.2 couple.2
  34.3 0.0 copy-start
  34.3 0.0 copy-start.1
  34.3 12.0 %all_to_all.37.refs_1_ = f32[16,64,128]{2,1,0:T(8,128)S(1)} all-to-all(f32[16,64,128]{2,1,0:T(8,128)S(1)} %couple.2), channel_id=1, replica_groups=mesh['z_lo'=2,'x'=4,'y_hi'=4,'y_lo'=2,'z_hi'=4,'core'=2] {'z_lo','x','y_..., dimensions={0} | all-to-all | bytes 1048576 | tf_op jit(solution)/shard_map/all_to_all | solution.py:412
  46.4 0.0 copy-done
  46.4 0.0 copy-done.1
  46.4 183.3 %turn.2 = (f32[64,256]{1,0:T(8,128)S(1)}, f32[64,256]{1,0:T(8,128)S(1)}, f32[2,64,256]{2,1,0:T(8,128)S(1)}, f32[64,256]{1,0:T(8,128)S(1)}) custom-call(s32[2,8]{1,0:T(2,128)S(1)} %copy-done.1, f32[16,64,128]{2,1,0:T(8,128)S(1)} %all_to_all.37.refs_1_, f32[64,1024]{1,0:T(8,128)S(1)} %copy-done), custom_call_target="tpu_custom_call" | custom-call | tf_op jit(solution)/shard_map/turn/pallas_call | solution.py:388
  229.7 5.5 collective-permute-start
  235.2 4.0 all_to_all.38.refs_3_.refs_4_
  239.2 0.0 collective-permute-done.refs_4_.refs_5_
  239.2 0.4 gram.1
  239.6 14.7 %all_to_all.39 = f32[16,17,4,128]{3,2,1,0:T(4,128)S(1)} all-to-all(f32[16,17,4,128]{3,2,1,0:T(4,128)S(1)} %bitcast.11), channel_id=1, replica_groups=mesh['z_lo'=2,'x'=4,'y_hi'=4,'y_lo'=2,'z_hi'=4,'core'=2] {'z_lo','x','y_..., dimensions={0} | all-to-all | bytes 1114112 | tf_op jit(solution)/shard_map/all_to_all | solution.py:406
  254.4 11.0 %all_to_all.40 = f32[4,17,4,128]{3,2,1,0:T(4,128)S(1)} all-to-all(f32[4,17,4,128]{3,2,1,0:T(4,128)S(1)} %bitcast.14), channel_id=1, replica_groups=mesh['z_lo'=2,'x'=4,'y_hi'=4,'y_lo'=2,'z_hi'=4,'core'=2] {'y_hi'}, dimensions={0} | all-to-all | bytes 278528 | tf_op jit(solution)/shard_map/all_to_all | solution.py:406
  265.4 0.2 couple.3
  265.6 12.6 %all_to_all.41.refs_1_ = f32[16,64,128]{2,1,0:T(8,128)S(1)} all-to-all(f32[16,64,128]{2,1,0:T(8,128)S(1)} %couple.3), channel_id=1, replica_groups=mesh['z_lo'=2,'x'=4,'y_hi'=4,'y_lo'=2,'z_hi'=4,'core'=2] {'z_lo','x','y_..., dimensions={0} | all-to-all | bytes 1048576 | tf_op jit(solution)/shard_map/all_to_all | solution.py:412
  278.2 285.0 %turn.3 = f32[64,1024]{1,0:T(8,128)} custom-call(s32[2,8]{1,0:T(2,128)S(1)} %copy-done.1, f32[16,64,128]{2,1,0:T(8,128)S(1)} %all_to_all.41.refs_1_, f32[64,256]{1,0:T(8,128)S(1)} %get-tuple-element.9.refs_1_.refs_2_, f32[64,256]{1,0:T(8,128)S(1)} %get-tuple-element.10.refs_2_.refs_3_, f32[2,64,256]{2,1,0:T(8,128)S(1)} %all_to_all.38.refs_3_.refs_4_, ...), custom_call_target="tpu_custom_call" | custom-call | tf_op jit(solution)/shard_map/turn/pallas_call | solution.py:388
  (2 shorter events, 0.1 us)
Async XLA Ops:
  34.3 12.0 %copy-start = (f32[64,1024]{1,0:T(8,128)S(1)}, f32[64,1024]{1,0:T(8,128)}, u32[]{:S(2)}) copy-start(f32[64,1024]{1,0:T(8,128)} %refs_2_.1) | copy-start | bytes 786436
  34.3 12.0 %copy-start.1 = (s32[2,8]{1,0:T(2,128)S(1)}, s32[2,8]{1,0:T(2,128)}, u32[]{:S(2)}) copy-start(s32[2,8]{1,0:T(2,128)} %refs_0_.5) | copy-start | bytes 196
  229.7 9.6 %collective-permute-start = (f32[64,256]{1,0:T(8,128)S(1)}, f32[64,256]{1,0:T(8,128)S(1)}, u32[]{:S(2)}, u32[]{:S(2)}) collective-permute-start(f32[64,256]{1,0:T(8,128)S(1)} %get-tuple-element.12), channel_id=1, source_target_pairs={{0,7},{1,2},{2,1},{3,4},{4,3},{5,6},{6,5},{7,0},{8,15},{9,10},{10,... | collective-permute-start | bytes 196616 | tf_op jit(solution)/shard_map/ppermute | solution.py:419

commit v6 on v5

--- a/solution.py
+++ b/solution.py
@@ -17,7 +17,7 @@
 BANDS = WIDTH // PART
 NORMS = 2 * PART
 FULL = NORMS + 4
-OUTER = ("z_lo", "x", "y_lo")
+OUTER = ("x", "z_lo", "y_lo")
 RING = ("y_hi",)
 COL = ("z_hi", "core")
 CORE = "core"

time: 564 us -> 563 us (level)
  the two profiles are of different devices: /device:TPU:8 before, /device:TPU:128 now
where the time goes in v6:
time: 563 us
  Pallas kernels  471 us (84%)
  blocking collectives  90.5 us (16%)
    pallas_call x2, Pallas kernels, turn(): pl.pallas_call(lambda *refs: turn_kernel(step, *refs), out_shape=outs, in...  468 us
    all_to_all x4, blocking collectives, exchange(): parts = lax.all_to_all(parts.reshape(count, FULL // 4, 4, HALF), axes, 0, 0)  60 us
    all_to_all x2, blocking collectives, whole(): return lax.all_to_all(couple(exchange(parts, RING)), OUTER, 0, 0)  22.6 us
  transfers between devices with their start and end apart: 1, of which 0 were waited for; matrix products, arithmetic and copies ran while one was open for 0% of the time, Pallas kernels for 0%

profile of v6, /device:TPU:128, one launch (start us, length us, event | category | flops | bytes accessed | tf_op | source)
XLA Modules:
  0.0 563.1 jit_solution(15572553441404124741)
XLA Ops:
  0.0 1.4 first_gram.1
  1.4 18.4 %all_to_all.35 = f32[16,17,4,128]{3,2,1,0:T(4,128)S(1)} all-to-all(f32[16,17,4,128]{3,2,1,0:T(4,128)S(1)} %bitcast.10), channel_id=1, replica_groups=mesh['z_lo'=2,'x'=4,'y_hi'=4,'y_lo'=2,'z_hi'=4,'core'=2] {'x','z_lo','y_..., dimensions={0} | all-to-all | bytes 1114112 | tf_op jit(solution)/shard_map/all_to_all | solution.py:406
  19.9 14.4 %all_to_all.36 = f32[4,17,4,128]{3,2,1,0:T(4,128)S(1)} all-to-all(f32[4,17,4,128]{3,2,1,0:T(4,128)S(1)} %bitcast.12), channel_id=1, replica_groups=mesh['z_lo'=2,'x'=4,'y_hi'=4,'y_lo'=2,'z_hi'=4,'core'=2] {'y_hi'}, dimensions={0} | all-to-all | bytes 278528 | tf_op jit(solution)/shard_map/all_to_all | solution.py:406
  34.3 0.2 couple.2
  34.6 0.0 copy-start
  34.6 0.0 copy-start.1
  34.6 11.4 %all_to_all.37.refs_1_ = f32[16,64,128]{2,1,0:T(8,128)S(1)} all-to-all(f32[16,64,128]{2,1,0:T(8,128)S(1)} %couple.2), channel_id=1, replica_groups=mesh['z_lo'=2,'x'=4,'y_hi'=4,'y_lo'=2,'z_hi'=4,'core'=2] {'x','z_lo','y_..., dimensions={0} | all-to-all | bytes 1048576 | tf_op jit(solution)/shard_map/all_to_all | solution.py:412
  46.0 0.0 copy-done
  46.0 0.0 copy-done.1
  46.0 183.3 %turn.2 = (f32[64,256]{1,0:T(8,128)S(1)}, f32[64,256]{1,0:T(8,128)S(1)}, f32[2,64,256]{2,1,0:T(8,128)S(1)}, f32[64,256]{1,0:T(8,128)S(1)}) custom-call(s32[2,8]{1,0:T(2,128)S(1)} %copy-done.1, f32[16,64,128]{2,1,0:T(8,128)S(1)} %all_to_all.37.refs_1_, f32[64,1024]{1,0:T(8,128)S(1)} %copy-done), custom_call_target="tpu_custom_call" | custom-call | tf_op jit(solution)/shard_map/turn/pallas_call | solution.py:388
  229.3 1.9 collective-permute-start
  231.3 7.9 %all_to_all.38.refs_3_.refs_4_ = f32[2,64,256]{2,1,0:T(8,128)S(1)} all-to-all(f32[2,64,256]{2,1,0:T(8,128)S(1)} %get-tuple-element.11), channel_id=1, replica_groups=mesh['z_lo'=2,'x'=4,'y_hi'=4,'y_lo'=2,'z_hi'=4,'core'=2] {'core'}, dimensions={0} | all-to-all | bytes 262144 | tf_op jit(solution)/shard_map/all_to_all | solution.py:420
  239.2 0.0 collective-permute-done.refs_4_.refs_5_
  239.2 0.4 gram.1
  239.6 15.9 %all_to_all.39 = f32[16,17,4,128]{3,2,1,0:T(4,128)S(1)} all-to-all(f32[16,17,4,128]{3,2,1,0:T(4,128)S(1)} %bitcast.11), channel_id=1, replica_groups=mesh['z_lo'=2,'x'=4,'y_hi'=4,'y_lo'=2,'z_hi'=4,'core'=2] {'x','z_lo','y_..., dimensions={0} | all-to-all | bytes 1114112 | tf_op jit(solution)/shard_map/all_to_all | solution.py:406
  255.5 11.2 %all_to_all.40 = f32[4,17,4,128]{3,2,1,0:T(4,128)S(1)} all-to-all(f32[4,17,4,128]{3,2,1,0:T(4,128)S(1)} %bitcast.14), channel_id=1, replica_groups=mesh['z_lo'=2,'x'=4,'y_hi'=4,'y_lo'=2,'z_hi'=4,'core'=2] {'y_hi'}, dimensions={0} | all-to-all | bytes 278528 | tf_op jit(solution)/shard_map/all_to_all | solution.py:406
  266.7 0.2 couple.3
  267.0 11.1 %all_to_all.41.refs_1_ = f32[16,64,128]{2,1,0:T(8,128)S(1)} all-to-all(f32[16,64,128]{2,1,0:T(8,128)S(1)} %couple.3), channel_id=1, replica_groups=mesh['z_lo'=2,'x'=4,'y_hi'=4,'y_lo'=2,'z_hi'=4,'core'=2] {'x','z_lo','y_..., dimensions={0} | all-to-all | bytes 1048576 | tf_op jit(solution)/shard_map/all_to_all | solution.py:412
  278.1 285.0 %turn.3 = f32[64,1024]{1,0:T(8,128)} custom-call(s32[2,8]{1,0:T(2,128)S(1)} %copy-done.1, f32[16,64,128]{2,1,0:T(8,128)S(1)} %all_to_all.41.refs_1_, f32[64,256]{1,0:T(8,128)S(1)} %get-tuple-element.9.refs_1_.refs_2_, f32[64,256]{1,0:T(8,128)S(1)} %get-tuple-element.10.refs_2_.refs_3_, f32[2,64,256]{2,1,0:T(8,128)S(1)} %all_to_all.38.refs_3_.refs_4_, ...), custom_call_target="tpu_custom_call" | custom-call | tf_op jit(solution)/shard_map/turn/pallas_call | solution.py:388
  (2 shorter events, 0.1 us)
Async XLA Ops:
  34.6 11.5 %copy-start = (f32[64,1024]{1,0:T(8,128)S(1)}, f32[64,1024]{1,0:T(8,128)}, u32[]{:S(2)}) copy-start(f32[64,1024]{1,0:T(8,128)} %refs_2_.1) | copy-start | bytes 786436
  34.6 11.5 %copy-start.1 = (s32[2,8]{1,0:T(2,128)S(1)}, s32[2,8]{1,0:T(2,128)}, u32[]{:S(2)}) copy-start(s32[2,8]{1,0:T(2,128)} %refs_0_.5) | copy-start | bytes 196
  229.3 9.9 %collective-permute-start = (f32[64,256]{1,0:T(8,128)S(1)}, f32[64,256]{1,0:T(8,128)S(1)}, u32[]{:S(2)}, u32[]{:S(2)}) collective-permute-start(f32[64,256]{1,0:T(8,128)S(1)} %get-tuple-element.12), channel_id=1, source_target_pairs={{0,7},{1,2},{2,1},{3,4},{4,3},{5,6},{6,5},{7,0},{8,15},{9,10},{10,... | collective-permute-start | bytes 196616 | tf_op jit(solution)/shard_map/ppermute | solution.py:419

commit v7 on v6

--- a/solution.py
+++ b/solution.py
@@ -136,14 +136,18 @@
         copy.start()
     for copy in copies:
         copy.wait()
-    gram_kernel(0, pairing, slab, out, blocks)
+    write_gram(pairing[0, lax.axis_index(COL)], (slab,), out, blocks)
 
 
 def gram_kernel(step, pairing_ref, *refs):
     *ins, out, blocks = refs
+    write_gram(pick(pairing_ref, step), ins, out, blocks)
+
+
+def write_gram(which, ins, out, blocks):
     load_blocks(ins, blocks)
     norms = []
-    for pair, (f, s) in enumerate(slots_of(pick(pairing_ref, step))):
+    for pair, (f, s) in enumerate(slots_of(which)):
         x = blocks[f]
         y = blocks[s]
         xh, xl = halves(x)
@@ -198,8 +202,20 @@
 
 def turn_kernel(step, pairing_ref, gram, *refs):
     count = 1 if step == 0 else 4
-    ins, outs, (blocks, coupling, powers, solved) = refs[:count], refs[count:-4], refs[-4:]
+    ins, outs, (blocks, coupling, powers, solved, done, sems) = refs[:count], refs[count:-6], refs[-6:]
     load_blocks(ins, blocks)
+
+    def finish(pair, side, slot, value):
+        if step == 0:
+            blocks[slot] = value
+            return []
+        index = 2 * pair + side
+        done[index] = value
+        dest = outs[0].at[:, pl.ds(pl.multiple_of(slot * WIDTH, WIDTH), WIDTH)]
+        copy = pltpu.make_async_copy(done.at[index], dest, sems.at[index])
+        copy.start()
+        return [copy]
+
     pairs = slots_of(pick(pairing_ref, step))
     xs, ys, cs, ms, ts, starts, m_squares = [], [], [], [], [], [], []
     bound = None
@@ -280,10 +296,14 @@
 
         tops = dots3([(halves(solved[pair]), squares[pair]) for pair in range(2)], NN)
         zs = [(unit * zeroth) * z + (unit * first) * zr + t for z, zr, t in zip(zs, zrs, tops)]
+        copies = []
+        for pair, (f, _) in enumerate(pairs):
+            copies += finish(pair, 0, f, 2.0 * zs[pair] - xs[pair])
         zcs = dots3([(halves(z), c) for z, c in zip(zs, cs)], NN)
-        for (f, s), x, y, z, zc in zip(pairs, xs, ys, zs, zcs):
-            blocks[f] = 2.0 * z - x
-            blocks[s] = y + 2.0 * zc
+        for pair, (_, s) in enumerate(pairs):
+            copies += finish(pair, 1, s, ys[pair] + 2.0 * zcs[pair])
+        for copy in copies:
+            copy.wait()
 
     @pl.when(bound > SQUARINGS[-1][1])
     def _():
@@ -293,6 +313,7 @@
         relax = 2.0 / (2.0 + b)
         omega = 2.0 / (1.0 + relax * jnp.sqrt(1.0 + b))
         gain = omega * relax
+        copies = []
         for pair, (f, s) in enumerate(pairs):
             x = blocks[f]
             y = blocks[s]
@@ -306,13 +327,12 @@
                 return before + omega * (z - before) + gain * residual, z
 
             z, _ = lax.fori_loop(0, count_of(bound, STEPS), body, (relax * t, jnp.zeros_like(t)))
-            blocks[f] = 2.0 * z - x
-            blocks[s] = y + 2.0 * dot(z, c, NN)
-
-    if len(outs) == 1:
-        for s in range(4):
-            outs[0][:, s * WIDTH : (s + 1) * WIDTH] = blocks[s]
-    else:
+            copies += finish(pair, 0, f, 2.0 * z - x)
+            copies += finish(pair, 1, s, y + 2.0 * dot(z, c, NN))
+        for copy in copies:
+            copy.wait()
+
+    if step == 0:
         low, high, near, far = outs
         core = lax.axis_index(CORE)
         low[...] = blocks[0]
@@ -339,7 +359,7 @@
         out_specs=VMEM,
         scratch_shapes=[
             BLOCKS,
-            pltpu.VMEM(pairing.shape, pairing.dtype),
+            pltpu.SMEM(pairing.shape, pairing.dtype),
             pltpu.VMEM(slab.shape, slab.dtype),
             pltpu.SemaphoreType.DMA((2,)),
         ],
@@ -389,12 +409,14 @@
         lambda *refs: turn_kernel(step, *refs),
         out_shape=outs,
         in_specs=[VMEM] * (2 + len(ins)),
-        out_specs=[VMEM] * 4 if step == 0 else VMEM,
+        out_specs=[VMEM] * 4 if step == 0 else HBM,
         scratch_shapes=[
             BLOCKS,
             pltpu.VMEM((2, WIDTH, WIDTH), jnp.float32),
             pltpu.VMEM((2, WIDTH, WIDTH), jnp.float32),
             pltpu.VMEM((2, ROWS, WIDTH), jnp.float32),
+            BLOCKS,
+            pltpu.SemaphoreType.DMA((4,)),
         ],
         compiler_params=PARAMS,
         name="turn",

time: 563 us -> 563 us (level)
  the two profiles are of different devices: /device:TPU:128 before, /device:TPU:8 now
where the time goes in v7:
time: 563 us; the launch traced here: 562 us
  Pallas kernels  470 us (83%)
  blocking collectives  86.5 us (15%)
    pallas_call x2, Pallas kernels, turn(): pl.pallas_call(lambda *refs: turn_kernel(step, *refs), out_shape=outs, in...  468 us
    all_to_all x4, blocking collectives, exchange(): parts = lax.all_to_all(parts.reshape(count, FULL // 4, 4, HALF), axes, 0, 0)  58.9 us
    all_to_all x2, blocking collectives, whole(): return lax.all_to_all(couple(exchange(parts, RING)), OUTER, 0, 0)  23.4 us
  transfers between devices with their start and end apart: 1, of which 0 were waited for; matrix products, arithmetic and copies ran while one was open for 0% of the time, Pallas kernels for 0%

profile of v7, /device:TPU:8, one launch (start us, length us, event | category | flops | bytes accessed | tf_op | source)
XLA Modules:
  0.0 561.9 jit_solution(10100559396323297492)
XLA Ops:
  0.0 1.3 first_gram.1
  1.3 17.5 %all_to_all.35 = f32[16,17,4,128]{3,2,1,0:T(4,128)S(1)} all-to-all(f32[16,17,4,128]{3,2,1,0:T(4,128)S(1)} %bitcast.10), channel_id=1, replica_groups=mesh['z_lo'=2,'x'=4,'y_hi'=4,'y_lo'=2,'z_hi'=4,'core'=2] {'x','z_lo','y_..., dimensions={0} | all-to-all | bytes 1114112 | tf_op jit(solution)/shard_map/all_to_all | solution.py:428
  18.8 15.0 %all_to_all.36 = f32[4,17,4,128]{3,2,1,0:T(4,128)S(1)} all-to-all(f32[4,17,4,128]{3,2,1,0:T(4,128)S(1)} %bitcast.12), channel_id=1, replica_groups=mesh['z_lo'=2,'x'=4,'y_hi'=4,'y_lo'=2,'z_hi'=4,'core'=2] {'y_hi'}, dimensions={0} | all-to-all | bytes 278528 | tf_op jit(solution)/shard_map/all_to_all | solution.py:428
  33.8 0.2 couple.2
  34.0 0.0 copy-start
  34.0 0.0 copy-start.1
  34.1 11.6 %all_to_all.37.refs_1_ = f32[16,64,128]{2,1,0:T(8,128)S(1)} all-to-all(f32[16,64,128]{2,1,0:T(8,128)S(1)} %couple.2), channel_id=1, replica_groups=mesh['z_lo'=2,'x'=4,'y_hi'=4,'y_lo'=2,'z_hi'=4,'core'=2] {'x','z_lo','y_..., dimensions={0} | all-to-all | bytes 1048576 | tf_op jit(solution)/shard_map/all_to_all | solution.py:434
  45.7 0.0 copy-done
  45.7 0.0 copy-done.1
  45.7 183.3 %turn.2 = (f32[64,256]{1,0:T(8,128)S(1)}, f32[64,256]{1,0:T(8,128)S(1)}, f32[2,64,256]{2,1,0:T(8,128)S(1)}, f32[64,256]{1,0:T(8,128)S(1)}) custom-call(s32[2,8]{1,0:T(2,128)S(1)} %copy-done.1, f32[16,64,128]{2,1,0:T(8,128)S(1)} %all_to_all.37.refs_1_, f32[64,1024]{1,0:T(8,128)S(1)} %copy-done), custom_call_target="tpu_custom_call" | custom-call | tf_op jit(solution)/shard_map/turn/pallas_call | solution.py:408
  229.0 5.4 collective-permute-start
  234.4 4.1 all_to_all.38.refs_3_.refs_4_
  238.6 0.0 collective-permute-done.refs_4_.refs_5_
  238.6 0.4 gram.1
  239.0 15.1 %all_to_all.39 = f32[16,17,4,128]{3,2,1,0:T(4,128)S(1)} all-to-all(f32[16,17,4,128]{3,2,1,0:T(4,128)S(1)} %bitcast.11), channel_id=1, replica_groups=mesh['z_lo'=2,'x'=4,'y_hi'=4,'y_lo'=2,'z_hi'=4,'core'=2] {'x','z_lo','y_..., dimensions={0} | all-to-all | bytes 1114112 | tf_op jit(solution)/shard_map/all_to_all | solution.py:428
  254.1 11.3 %all_to_all.40 = f32[4,17,4,128]{3,2,1,0:T(4,128)S(1)} all-to-all(f32[4,17,4,128]{3,2,1,0:T(4,128)S(1)} %bitcast.14), channel_id=1, replica_groups=mesh['z_lo'=2,'x'=4,'y_hi'=4,'y_lo'=2,'z_hi'=4,'core'=2] {'y_hi'}, dimensions={0} | all-to-all | bytes 278528 | tf_op jit(solution)/shard_map/all_to_all | solution.py:428
  265.5 0.2 couple.3
  265.7 11.8 %all_to_all.41.refs_1_ = f32[16,64,128]{2,1,0:T(8,128)S(1)} all-to-all(f32[16,64,128]{2,1,0:T(8,128)S(1)} %couple.3), channel_id=1, replica_groups=mesh['z_lo'=2,'x'=4,'y_hi'=4,'y_lo'=2,'z_hi'=4,'core'=2] {'x','z_lo','y_..., dimensions={0} | all-to-all | bytes 1048576 | tf_op jit(solution)/shard_map/all_to_all | solution.py:434
  277.5 284.4 %turn.3 = f32[64,1024]{1,0:T(8,128)} custom-call(s32[2,8]{1,0:T(2,128)S(1)} %copy-done.1, f32[16,64,128]{2,1,0:T(8,128)S(1)} %all_to_all.41.refs_1_, f32[64,256]{1,0:T(8,128)S(1)} %get-tuple-element.9.refs_1_.refs_2_, f32[64,256]{1,0:T(8,128)S(1)} %get-tuple-element.10.refs_2_.refs_3_, f32[2,64,256]{2,1,0:T(8,128)S(1)} %all_to_all.38.refs_3_.refs_4_, ...), custom_call_target="tpu_custom_call" | custom-call | tf_op jit(solution)/shard_map/turn/pallas_call | solution.py:408
  (2 shorter events, 0.1 us)
Async XLA Ops:
  34.0 11.6 %copy-start = (f32[64,1024]{1,0:T(8,128)S(1)}, f32[64,1024]{1,0:T(8,128)}, u32[]{:S(2)}) copy-start(f32[64,1024]{1,0:T(8,128)} %refs_2_.1) | copy-start | bytes 786436
  34.0 11.6 %copy-start.1 = (s32[2,8]{1,0:T(2,128)S(1)}, s32[2,8]{1,0:T(2,128)}, u32[]{:S(2)}) copy-start(s32[2,8]{1,0:T(2,128)} %refs_0_.5) | copy-start | bytes 196
  229.0 9.6 %collective-permute-start = (f32[64,256]{1,0:T(8,128)S(1)}, f32[64,256]{1,0:T(8,128)S(1)}, u32[]{:S(2)}, u32[]{:S(2)}) collective-permute-start(f32[64,256]{1,0:T(8,128)S(1)} %get-tuple-element.12), channel_id=1, source_target_pairs={{0,7},{1,2},{2,1},{3,4},{4,3},{5,6},{6,5},{7,0},{8,15},{9,10},{10,... | collective-permute-start | bytes 196616 | tf_op jit(solution)/shard_map/ppermute | solution.py:441
